TPU v7x, 512 devices: a whole 4x8x8 slice. The times are simulated.
512 devices in a mesh: grp: 16 (over z_lo, x), mem: 32 (over y, z_hi, core).
Axes of the slice: x: 4, y: 8, z: 8 (z_hi: 2, z_lo: 4; z = z_hi * 4 + z_lo), core: 2. Of those that a mesh axis runs over, the one named last changes fastest.
Arguments:
- points: float32 [8192, 128], P(('grp', 'mem')), may hold values from -40 to 40, as said below
- slab: float32 [65536, 128], P('mem'), may hold values from -40 to 40, as said below
Outputs:
- new_points: float32 [8192, 128], P(('grp', 'mem'))
Inputs may be any that keep to these rules, and one draw needn't show every extreme that they name: Support points lie near the chains' centres. `slab`: each block of 2048 rows is one chain with its own centre and scale.
All inputs are finite; a program needn't handle non-finite values.
Results may differ from a plain program's by a relative error of at most 0.0001.
Values sent between devices are 32-bit elements; how exact they have to be, the bound alone decides.
No kernel may reach another device: no remote copies, remote signals or barrier semaphores. Data moves between devices by JAX's collectives and lax.ppermute only.
A program may use at most 64 MiB of HBM per device.

v0:
```python
import jax
import jax.numpy as jnp
from jax import lax
from jax.sharding import PartitionSpec as P


def weights_of(left, right_operand):
    left_square_norm = jnp.sum(jnp.square(left), axis=1)
    right_square_norm = jnp.sum(jnp.square(right_operand), axis=1)
    cross_product = jnp.dot(
        left, right_operand.T, precision=lax.Precision.HIGHEST, preferred_element_type=jnp.float32
    )
    squared_distance = left_square_norm[:, None] + right_square_norm[None, :] - 2.0 * cross_product
    return 1.0 / jnp.sqrt(squared_distance + 1.0)


def pair_terms(anchors, piece):
    wts = weights_of(anchors, piece)
    pair_vec = jnp.dot(
        wts, piece, precision=lax.Precision.HIGHEST, preferred_element_type=jnp.float32
    )
    pair_sum = jnp.sum(wts, axis=1)
    return (pair_vec, pair_sum)


def shards(points, slab):
    owned = points.shape[0]
    width = points.shape[1]
    samp_rows = slab.shape[0]
    groups = lax.axis_size("grp")
    ratio = samp_rows / (owned * groups)
    group = lax.all_gather(points, "mem", axis=0, tiled=True)
    sblock = min(samp_rows, 512)
    slab_blocks = slab.reshape(samp_rows // sblock, sblock, width)

    def attract_step(carry, rows):
        numer, total = carry
        wts = weights_of(group, rows)
        numer = numer + jnp.dot(
            wts, rows, precision=lax.Precision.HIGHEST, preferred_element_type=jnp.float32
        )
        total = total + jnp.sum(wts, axis=1)
        return ((numer, total), None)

    init = (
        jnp.zeros((group.shape[0], width), jnp.float32),
        jnp.zeros((group.shape[0],), jnp.float32),
    )
    (numer, total), _ = lax.scan(attract_step, init, slab_blocks)
    numer_all, total_all = lax.psum((numer, total), "mem")
    first = lax.axis_index("mem") * owned
    numer_own = lax.dynamic_slice_in_dim(numer_all, first, owned, 0)
    total_own = lax.dynamic_slice_in_dim(total_all, first, owned, 0)
    pair_vec, pair_sum = pair_terms(
        points, lax.all_gather(points, ("grp", "mem"), axis=0, tiled=True)
    )
    repel = points * pair_sum[:, None] - pair_vec
    update_output = (ratio * repel + numer_own) / total_own[:, None]
    return update_output


def solution(mesh):
    placed = (P(("grp", "mem"), None), P("mem", None))
    return jax.shard_map(
        shards, mesh=mesh, in_specs=placed, out_specs=P(("grp", "mem"), None), check_vma=False
    )
```

profile of v0, /device:TPU:1, one launch (start us, length us, event | category | flops | bytes accessed | tf_op | source)
XLA Modules:
  0.0 837.4 jit_solution(9507223085409808582)
XLA Ops:
  7.4 0.0 all-gather.2.cloned.1.call-start
  7.4 0.7 all-gather.2.cloned.1.call-update
  8.1 0.0 all-reduce.2.cloned.1.call-start
  8.2 60.6 %all_gather.7 = f32[512,128]{1,0:T(8,128)S(1)} all-gather(f32[16,128]{1,0:T(8,128)} %param.4), channel_id=1, replica_groups=mesh['grp'=16,'mem'=32] {'mem'}, dimensions={0}, use_global_device_ids=true | all-gather | bytes 270336 | tf_op jit(solution)/shard_map/all_gather | solution.py:32
  68.8 0.1 multiply_reduce_fusion.1
  68.9 0.0 copy-start.2
  69.0 24.2 %while.15 = (s32[]{:T(128)}, f32[512,128]{1,0:T(8,128)S(1)}, f32[512]{0:T(512)S(1)}, f32[512]{0:T(512)S(1)}, f32[4,512,128]{2,1,0:T(8,128)}, /*index=5*/f32[512,128]{1,0:T(8,128)S(1)}, s32[]{:T(128)}, s32[]{:T(128)}) while((s32[]{:T(128)}, f32[512,128]{1,0:T(8,128)S(1)}, f32[512]{0:T(512)S(1)}, f32[512]{0:T(512)S(1)}, ...), condition=%wide.region_7.8_spmd.clone, body=%wide.region_4.7_spmd.clone.sunk | while | flops 806879232 | bytes 3685476 | solution.py:49
  69.0 1.1 fusion.33
  70.1 2.1 fusion.34
  72.2 2.8 convolution_add_fusion.2
  75.0 1.1 fusion.33
  76.1 2.1 fusion.34
  78.2 2.8 convolution_add_fusion.2
  81.1 1.1 fusion.33
  82.2 2.1 fusion.34
  84.3 2.8 convolution_add_fusion.2
  87.1 1.1 fusion.33
  88.2 2.1 fusion.34
  90.3 2.8 convolution_add_fusion.2
  93.2 0.0 copy-start.1
  93.2 0.7 copy-done.1
  93.9 0.0 all-reduce.2.cloned.1.call-update
  93.9 0.0 copy-done.2
  93.9 0.1 multiply_reduce_fusion.2
  94.0 84.0 %psum.15 = f32[512]{0:T(512)S(1)} all-reduce(f32[512]{0:T(512)S(1)} %get-tuple-element.73), channel_id=1, replica_groups=mesh['grp'=16,'mem'=32] {'mem'}, use_global_device_ids=true, to_apply=%region_9.10 | all-reduce | flops 512 | bytes 4096 | tf_op jit(solution)/shard_map/psum | solution.py:50
  178.0 0.1 dynamic_slice.13
  178.1 640.2 %all-gather.2.cloned.1.call-done = f32[8192,128]{1,0:T(8,128)} async-done(((f32[16,128]{1,0:T(8,128)}), f32[8192,128]{1,0:T(8,128)}) %all-gather.2.cloned.1.call-update) | async-done | bytes 4194320 | tf_op jit(solution)/shard_map/all_gather | solution.py:55
  818.3 0.0 copy-start
  818.3 3.5 multiply_reduce_fusion
  821.8 0.0 copy-done
  821.8 3.6 fusion.18
  825.4 0.0 all-reduce.2.cloned.1.call-done
  825.4 4.5 fusion.16
  (6 shorter events, 0.1 us)
Async XLA Ops:
  7.4 810.9 %all-gather.2.cloned.1.call-start = ((), (), s32[]{:S(2)}) async-start(), calls=%async_computation | async-start | bytes 4202496 | tf_op jit(solution)/shard_map/all_gather | solution.py:55
  8.1 817.3 %all-reduce.2.cloned.1.call-start = ((), (), s32[]{:S(2)}) async-start(), calls=%async_computation.1 | async-start | bytes 524288 | tf_op jit(solution)/shard_map/psum | solution.py:50
  68.9 24.9 %copy-start.2 = (f32[16,128]{1,0:T(8,128)S(1)}, f32[16,128]{1,0:T(8,128)}, u32[]{:S(2)}) copy-start(f32[16,128]{1,0:T(8,128)} %param.4) | copy-start | bytes 24580
  93.2 0.7 copy-start.1
  818.3 3.5 copy-start
Sparse Core Ops, SparseCore 0:
  10.4 807.8 all-gather.1
Sparse Core Ops, SparseCore 1:
  94.0 337.4 all-reduce.1
where the time goes:
time: 843 us; the launch traced here: 837 us
  waiting for transfers between devices  641 us (76%)
  blocking collectives  145 us (17%)
  matrix products  27.8 us (3%)
  between operations  14.9 us (2%)
    all_gather x1, waiting for transfers between devices, shards(): lax.all_gather(points, ('grp', 'mem'), axis=0, tiled=True)  640 us
    psum x1, blocking collectives, shards(): numer_all, total_all = lax.psum((numer, total), 'mem')  84 us
    all_gather x1, blocking collectives, shards(): group = lax.all_gather(points, 'mem', axis=0, tiled=True)  60.6 us
  transfers between devices with their start and end apart: 2, of which 1 were waited for; matrix products, arithmetic and copies ran while one was open for 4% of the time, Pallas kernels for 0%

commit v1 on v0

v1 whole, which is shorter than its diff:
```python
import functools

import jax
import jax.numpy as jnp
from jax import lax
from jax.experimental import pallas as pl
from jax.experimental.pallas import tpu as pltpu
from jax.sharding import PartitionSpec as P

F32, BF16 = jnp.float32, jnp.bfloat16
AXES = ("grp", "mem")
CHIPS_X, CHIPS_Y, Z_LO, Z_HI, CORES = 4, 8, 4, 2, 2
TILE = 512


def place(index):
    group, member = divmod(index, CHIPS_Y * Z_HI * CORES)
    z_lo, x = divmod(group, CHIPS_X)
    y, rest = divmod(member, Z_HI * CORES)
    z_hi, core = divmod(rest, CORES)
    return x, y, z_hi * Z_LO + z_lo, core


def index_of(x, y, z, core):
    z_hi, z_lo = divmod(z, Z_LO)
    return (z_lo * CHIPS_X + x) * CHIPS_Y * Z_HI * CORES + (y * Z_HI + z_hi) * CORES + core


def team_of(z):
    return z if z < Z_LO else (z - Z_LO) ^ 2


DEVICES = range(CHIPS_X * CHIPS_Y * Z_LO * Z_HI * CORES)
TEAMS = {}
for _i in DEVICES:
    _x, _y, _z, _c = place(_i)
    TEAMS.setdefault((_x, team_of(_z), _c), []).append(_i)
TEAMS = list(TEAMS.values())

Z_ORDER = ((0, 2, 1, 3, 4, 6, 5, 7), (1, 0, 3, 2, 6, 7, 4, 5))
CROSS = []
for _i in DEVICES:
    _x, _y, _z, _c = place(_i)
    CROSS.append((index_of((_x + _y) % CHIPS_X, _y, Z_ORDER[_y // CHIPS_X][_z], _c), _i))
SWAP = [(i, i ^ 1) for i in DEVICES]


def split2(v):
    hi = v.astype(BF16)
    return hi, (v - hi.astype(F32)).astype(BF16)


def split3(v):
    hi = v.astype(BF16).astype(F32)
    mid = (v - hi).astype(BF16).astype(F32)
    return hi, mid, v - hi - mid


def columns(first, second):
    ref = second if first is None else first
    lane = lax.broadcasted_iota(jnp.int32, (ref.shape[0], 128), 1)
    out = jnp.where(lane < 6, 1.0, 0.0).astype(F32)
    for at, col in ((0, first), (3, second)):
        if col is not None:
            for k, part in enumerate(split3(col)):
                out = jnp.where(lane == at + k, part, out)
    return out.astype(BF16)


NT = (((1,), (1,)), ((), ()))


def left_operands(pts):
    hi, lo = split2(-2.0 * pts)
    norm = jnp.sum(pts * pts, axis=1, keepdims=True) + 1.0
    return jnp.concatenate([hi, hi], axis=1), jnp.concatenate([lo, columns(None, norm)], axis=1)


def accumulate(left, rows, state):
    vec, tot = state
    hi, lo = split2(rows)
    norm = jnp.sum(rows * rows, axis=1, keepdims=True)
    both = jnp.concatenate([hi, lo], axis=1)
    extra = jnp.concatenate([hi, columns(norm, None)], axis=1)
    d = lax.dot_general(left[0], both, NT, preferred_element_type=F32)
    d = d + lax.dot_general(left[1], extra, NT, preferred_element_type=F32)
    w = lax.rsqrt(jnp.maximum(d, 1.0))
    w_hi, w_lo = split2(w)
    part = jnp.dot(w_hi, both, preferred_element_type=F32)
    part = part + jnp.dot(w_lo, both, preferred_element_type=F32)
    vec = vec + part
    for k in range(rows.shape[0] // 128):
        tot = tot + w[:, 128 * k : 128 * (k + 1)]
    return vec, tot


def slab_kernel(pts_ref, own_ref, other_ref, vec_ref, tot_ref):
    pts = pts_ref[...]
    left = left_operands(pts)
    state = (jnp.zeros((pts.shape[0], 256), F32), jnp.zeros((pts.shape[0], 128), F32))
    for ref in (own_ref, other_ref):
        for t in range(ref.shape[0] // TILE):
            state = accumulate(left, ref[t * TILE : (t + 1) * TILE, :], state)
    vec_ref[...] = state[0][:, :128] + state[0][:, 128:]
    tot_ref[...] = state[1]


def pair_kernel(ratio, pts_ref, first_ref, second_ref, vec_ref, tot_ref, out_ref):
    pts = pts_ref[...]
    left = left_operands(pts)
    state = (jnp.zeros((pts.shape[0], 256), F32), jnp.zeros((pts.shape[0], 128), F32))
    for ref in (first_ref, second_ref):
        state = accumulate(left, ref[...], state)
    pair_sum = jnp.sum(state[1], axis=1, keepdims=True)
    repel = pts * pair_sum - (state[0][:, :128] + state[0][:, 128:])
    numer = ratio * repel + vec_ref[...]
    weight = jnp.sum(tot_ref[...], axis=1, keepdims=True)
    lane = lax.broadcasted_iota(jnp.int32, (8, 128), 1)
    for k in range(out_ref.shape[0]):
        at = 16 * k
        out_ref[k, 0:16, :] = numer[at : at + 16]
        out_ref[k, 16:24, :] = jnp.where(lane < 64, weight[at : at + 8], weight[at + 8 : at + 16])


def final_kernel(parts_ref, out_ref):
    total = parts_ref[0]
    for k in range(1, parts_ref.shape[0]):
        total = total + parts_ref[k]
    out_ref[0:8, :] = total[0:8] / total[16:24, 0:1]
    out_ref[8:16, :] = total[8:16] / total[16:24, 127:128]


def call(kernel, shapes, flops, *args):
    return pl.pallas_call(
        kernel,
        out_shape=shapes,
        in_specs=[pl.BlockSpec(memory_space=pltpu.VMEM)] * len(args),
        out_specs=jax.tree.map(lambda _: pl.BlockSpec(memory_space=pltpu.VMEM), shapes),
        cost_estimate=pl.CostEstimate(flops=flops, bytes_accessed=1 << 20, transcendentals=1 << 20),
        compiler_params=pltpu.CompilerParams(vmem_limit_bytes=48 << 20),
    )(*args)


def shards(points, slab):
    owned, width = points.shape
    team = len(TEAMS[0])
    ratio = slab.shape[0] / (owned * lax.axis_size("grp"))
    other = lax.ppermute(slab, AXES, SWAP)
    copies = jnp.broadcast_to(points[None], (team, owned, width))
    pts = lax.all_to_all(copies, AXES, 0, 0, axis_index_groups=TEAMS).reshape(team * owned, width)
    far = lax.ppermute(pts, AXES, CROSS)
    sums = (
        jax.ShapeDtypeStruct((team * owned, width), F32),
        jax.ShapeDtypeStruct((team * owned, 128), F32),
    )
    vec, tot = call(slab_kernel, sums, 1 << 32, pts, slab, other)
    far_other = lax.ppermute(far, AXES, SWAP)
    block = jax.ShapeDtypeStruct((team, owned + 8, width), F32)
    part = call(functools.partial(pair_kernel, ratio), block, 1 << 28, pts, far, far_other, vec, tot)
    parts = lax.all_to_all(part, AXES, 0, 0, axis_index_groups=TEAMS)
    return call(final_kernel, jax.ShapeDtypeStruct((owned, width), F32), 1 << 16, parts)


def solution(mesh):
    placed = (P(("grp", "mem"), None), P("mem", None))
    return jax.shard_map(
        shards, mesh=mesh, in_specs=placed, out_specs=P(("grp", "mem"), None), check_vma=False
    )
```

time: 843 us -> 63.9 us (0.08)
  the two profiles are of different devices: /device:TPU:1 before, /device:TPU:76 now
where the time goes in v1:
time: 63.9 us; the launch traced here: 63.6 us
  blocking collectives  45.8 us (72%)
  waiting for transfers between devices  5.84 us (9%)
  starting transfers between devices  5.73 us (9%)
  Pallas kernels  4.3 us (7%)
  local copies, waits for them, and re-layouts  1.93 us (3%)
    all_to_all x1, blocking collectives, shards(): lax.all_to_all(copies, AXES, 0, 0, axis_index_groups=TEAMS)  25.5 us
    all_to_all x1, blocking collectives, shards(): parts = lax.all_to_all(part, AXES, 0, 0, axis_index_groups=TEAMS)  20.3 us
    ppermute x1, waiting for transfers between devices, shards(): far = lax.ppermute(pts, AXES, CROSS)  5.83 us
    pallas_call x3, Pallas kernels, call(): pl.pallas_call(kernel, out_shape=shapes, in_specs=[pl.BlockSpec(memory_sp...  4.3 us
    ppermute x1, starting transfers between devices, shards(): other = lax.ppermute(slab, AXES, SWAP)  1.91 us
    ppermute x1, starting transfers between devices, shards(): far = lax.ppermute(pts, AXES, CROSS)  1.91 us
    ppermute x1, starting transfers between devices, shards(): far_other = lax.ppermute(far, AXES, SWAP)  1.91 us
  transfers between devices with their start and end apart: 3, of which 1 were waited for; matrix products, arithmetic and copies ran while one was open for 1% of the time, Pallas kernels for 4%

profile of v1, /device:TPU:76, one launch (start us, length us, event | category | flops | bytes accessed | tf_op | source)
XLA Modules:
  0.0 63.6 jit_solution(4440899927165332324)
XLA Ops:
  0.0 1.9 %collective-permute-start.2 = (f32[2048,128]{1,0:T(8,128)}, f32[2048,128]{1,0:T(8,128)S(1)}, u32[]{:S(2)}, u32[]{:S(2)}) collective-permute-start(f32[2048,128]{1,0:T(8,128)} %own_ref.1), channel_id=1, source_target_pairs={{0,1},{1,0},{2,3},{3,2},{4,5},{5,4},{6,7},{7,6},{8,9},{9,8},{10,11... | collective-permute-start | bytes 3145736 | tf_op jit(solution)/shard_map/ppermute | solution.py:148
  1.9 0.7 %broadcast_in_dim.2 = f32[16,16,128]{2,1,0:T(8,128)S(1)} broadcast(f32[16,128]{1,0:T(8,128)} %param.2), dimensions={1,2} | broadcast | bytes 139264 | tf_op jit(solution)/shard_map/broadcast_in_dim | solution.py:149
  2.6 25.5 %all_to_all.10 = f32[16,16,128]{2,1,0:T(8,128)S(1)} all-to-all(f32[16,16,128]{2,1,0:T(8,128)S(1)} %broadcast_in_dim.2), channel_id=1, replica_groups={{0,4,8,12,16,20,24,28,258,262,266,270,274,278,282,286},{1,5,9,13,17,21,..., dimensions={0} | all-to-all | bytes 262144 | tf_op jit(solution)/shard_map/all_to_all | solution.py:150
  28.2 1.9 %collective-permute-start = (f32[256,128]{1,0:T(8,128)S(1)}, f32[256,128]{1,0:T(8,128)S(1)}, u32[]{:S(2)}, u32[]{:S(2)}) collective-permute-start(f32[256,128]{1,0:T(8,128)S(1)} %bitcast.1), channel_id=1, source_target_pairs={{0,0},{1,1},{2,2},{3,3},{36,4},{37,5},{38,6},{39,7},{72,8},{73,9},... | collective-permute-start | bytes 393224 | tf_op jit(solution)/shard_map/ppermute | solution.py:151
  30.1 5.8 %collective-permute-done.first_ref = f32[256,128]{1,0:T(8,128)S(1)} collective-permute-done((f32[256,128]{1,0:T(8,128)S(1)}, f32[256,128]{1,0:T(8,128)S(1)}, u32[]{:S(2)}, u32[]{:S(2)}) %collective-permute-start) | collective-permute-done | bytes 131104 | tf_op jit(solution)/shard_map/ppermute | solution.py:151
  35.9 1.9 %collective-permute-start.1 = (f32[256,128]{1,0:T(8,128)S(1)}, f32[256,128]{1,0:T(8,128)S(1)}, u32[]{:S(2)}, u32[]{:S(2)}) collective-permute-start(f32[256,128]{1,0:T(8,128)S(1)} %collective-permute-done.first_ref), channel_id=1, source_target_pairs={{0,1},{1,0},{2,3},{3,2},{4,5},{5,4},{6,7},{7,6},{8,9},{9,8},{10,11... | collective-permute-start | bytes 393224 | tf_op jit(solution)/shard_map/ppermute | solution.py:157
  37.8 0.0 collective-permute-done.2.other_ref
  37.8 0.0 copy-start
  37.9 1.2 %copy-done = f32[2048,128]{1,0:T(8,128)S(1)} copy-done((f32[2048,128]{1,0:T(8,128)S(1)}, f32[2048,128]{1,0:T(8,128)}, u32[]{:S(2)}) %copy-start) | copy-done | bytes 1048600
  39.1 2.7 %shard_map.28 = (f32[256,128]{1,0:T(8,128)S(1)}, f32[256,128]{1,0:T(8,128)S(1)}) custom-call(f32[256,128]{1,0:T(8,128)S(1)} %bitcast.2, f32[2048,128]{1,0:T(8,128)S(1)} %copy-done, f32[2048,128]{1,0:T(8,128)S(1)} %collective-permute-done.2.other_ref), custom_call_target="tpu_custom_call" | custom-call | flops 4294967296 | bytes 1048576 | tf_op jit(solution)/shard_map/pallas_call | solution.py:134
  41.8 0.0 collective-permute-done.1.second_ref
  41.8 0.9 %shard_map.29 = f32[16,24,128]{2,1,0:T(8,128)S(1)} custom-call(f32[256,128]{1,0:T(8,128)S(1)} %bitcast.3, f32[256,128]{1,0:T(8,128)S(1)} %collective-permute-done.first_ref, f32[256,128]{1,0:T(8,128)S(1)} %collective-permute-done.1.second_ref, f32[256,128]{1,0:T(8,128)S(1)} %get-tuple-element.7.vec_ref, f32[256,128]{1,0:T(8,128)S(1)} %get-tuple-element.8.tot_ref), custom_call_target="tpu_custom_call" | custom-call | flops 268435456 | bytes 1048576 | tf_op jit(solution)/shard_map/pallas_call | solution.py:134
  42.7 20.3 %all_to_all.11.parts_ref = f32[16,24,128]{2,1,0:T(8,128)S(1)} all-to-all(f32[16,24,128]{2,1,0:T(8,128)S(1)} %shard_map.29), channel_id=1, replica_groups={{0,4,8,12,16,20,24,28,258,262,266,270,274,278,282,286},{1,5,9,13,17,21,..., dimensions={0} | all-to-all | bytes 393216 | tf_op jit(solution)/shard_map/all_to_all | solution.py:160
  62.9 0.7 %shard_map.30 = f32[16,128]{1,0:T(8,128)} custom-call(f32[16,24,128]{2,1,0:T(8,128)S(1)} %all_to_all.11.parts_ref), custom_call_target="tpu_custom_call" | custom-call | flops 65536 | bytes 1048576 | tf_op jit(solution)/shard_map/pallas_call | solution.py:134
Async XLA Ops:
  0.0 37.8 %collective-permute-start.2 = (f32[2048,128]{1,0:T(8,128)}, f32[2048,128]{1,0:T(8,128)S(1)}, u32[]{:S(2)}, u32[]{:S(2)}) collective-permute-start(f32[2048,128]{1,0:T(8,128)} %own_ref.1), channel_id=1, source_target_pairs={{0,1},{1,0},{2,3},{3,2},{4,5},{5,4},{6,7},{7,6},{8,9},{9,8},{10,11... | collective-permute-start | bytes 3145736 | tf_op jit(solution)/shard_map/ppermute | solution.py:148
  28.2 7.7 %collective-permute-start = (f32[256,128]{1,0:T(8,128)S(1)}, f32[256,128]{1,0:T(8,128)S(1)}, u32[]{:S(2)}, u32[]{:S(2)}) collective-permute-start(f32[256,128]{1,0:T(8,128)S(1)} %bitcast.1), channel_id=1, source_target_pairs={{0,0},{1,1},{2,2},{3,3},{36,4},{37,5},{38,6},{39,7},{72,8},{73,9},... | collective-permute-start | bytes 393224 | tf_op jit(solution)/shard_map/ppermute | solution.py:151
  35.9 5.9 %collective-permute-start.1 = (f32[256,128]{1,0:T(8,128)S(1)}, f32[256,128]{1,0:T(8,128)S(1)}, u32[]{:S(2)}, u32[]{:S(2)}) collective-permute-start(f32[256,128]{1,0:T(8,128)S(1)} %collective-permute-done.first_ref), channel_id=1, source_target_pairs={{0,1},{1,0},{2,3},{3,2},{4,5},{5,4},{6,7},{7,6},{8,9},{9,8},{10,11... | collective-permute-start | bytes 393224 | tf_op jit(solution)/shard_map/ppermute | solution.py:157
  37.8 1.2 %copy-start = (f32[2048,128]{1,0:T(8,128)S(1)}, f32[2048,128]{1,0:T(8,128)}, u32[]{:S(2)}) copy-start(f32[2048,128]{1,0:T(8,128)} %own_ref.1) | copy-start | bytes 3145732

commit v2 on v1

--- a/solution.py
+++ b/solution.py
@@ -11,6 +11,8 @@
 AXES = ("grp", "mem")
 CHIPS_X, CHIPS_Y, Z_LO, Z_HI, CORES = 4, 8, 4, 2, 2
 TILE = 512
+HEAD = 1
+COST = (1 << 20, 1 << 34, 1 << 31)
 
 
 def place(index):
@@ -94,26 +96,41 @@
     return vec, tot
 
 
-def slab_kernel(pts_ref, own_ref, other_ref, vec_ref, tot_ref):
+def zeros(rows):
+    return jnp.zeros((rows, 256), F32), jnp.zeros((rows, 128), F32)
+
+
+def add_tiles(left, state, slab_ref, tiles):
+    for t in tiles:
+        state = accumulate(left, slab_ref[t * TILE : (t + 1) * TILE, :], state)
+    return state
+
+
+def head_kernel(pts_ref, slab_ref, left1_ref, left2_ref, vec_ref, tot_ref, held, sem):
+    copy = pltpu.make_async_copy(slab_ref.at[pl.ds(0, held.shape[0])], held, sem)
+    copy.start()
     pts = pts_ref[...]
     left = left_operands(pts)
-    state = (jnp.zeros((pts.shape[0], 256), F32), jnp.zeros((pts.shape[0], 128), F32))
-    for ref in (own_ref, other_ref):
-        for t in range(ref.shape[0] // TILE):
-            state = accumulate(left, ref[t * TILE : (t + 1) * TILE, :], state)
-    vec_ref[...] = state[0][:, :128] + state[0][:, 128:]
-    tot_ref[...] = state[1]
+    left1_ref[...], left2_ref[...] = left
+    copy.wait()
+    vec_ref[...], tot_ref[...] = add_tiles(left, zeros(pts.shape[0]), held, range(HEAD))
 
 
-def pair_kernel(ratio, pts_ref, first_ref, second_ref, vec_ref, tot_ref, out_ref):
+def rest_kernel(first, left1_ref, left2_ref, vec_in, tot_in, slab_ref, vec_ref, tot_ref):
+    left, state = (left1_ref[...], left2_ref[...]), (vec_in[...], tot_in[...])
+    tiles = range(first, slab_ref.shape[0] // TILE)
+    vec_ref[...], tot_ref[...] = add_tiles(left, state, slab_ref, tiles)
+
+
+def pair_kernel(ratio, pts_ref, left1_ref, left2_ref, first_ref, second_ref, vec_ref, tot_ref, out_ref):
     pts = pts_ref[...]
-    left = left_operands(pts)
-    state = (jnp.zeros((pts.shape[0], 256), F32), jnp.zeros((pts.shape[0], 128), F32))
+    left = left1_ref[...], left2_ref[...]
+    state = zeros(pts.shape[0])
     for ref in (first_ref, second_ref):
         state = accumulate(left, ref[...], state)
     pair_sum = jnp.sum(state[1], axis=1, keepdims=True)
     repel = pts * pair_sum - (state[0][:, :128] + state[0][:, 128:])
-    numer = ratio * repel + vec_ref[...]
+    numer = ratio * repel + (vec_ref[:, :128] + vec_ref[:, 128:])
     weight = jnp.sum(tot_ref[...], axis=1, keepdims=True)
     lane = lax.broadcasted_iota(jnp.int32, (8, 128), 1)
     for k in range(out_ref.shape[0]):
@@ -130,14 +147,17 @@
     out_ref[8:16, :] = total[8:16] / total[16:24, 127:128]
 
 
-def call(kernel, shapes, flops, *args):
+def call(kernel, shapes, flops, *args, hbm=(), scratch=()):
+    args = [pltpu.with_memory_space_constraint(a, pltpu.HBM) if k in hbm else a for k, a in enumerate(args)]
+    spaces = [pltpu.HBM if k in hbm else pltpu.VMEM for k in range(len(args))]
     return pl.pallas_call(
         kernel,
         out_shape=shapes,
-        in_specs=[pl.BlockSpec(memory_space=pltpu.VMEM)] * len(args),
+        in_specs=[pl.BlockSpec(memory_space=space) for space in spaces],
         out_specs=jax.tree.map(lambda _: pl.BlockSpec(memory_space=pltpu.VMEM), shapes),
-        cost_estimate=pl.CostEstimate(flops=flops, bytes_accessed=1 << 20, transcendentals=1 << 20),
-        compiler_params=pltpu.CompilerParams(vmem_limit_bytes=48 << 20),
+        scratch_shapes=scratch,
+        cost_estimate=pl.CostEstimate(flops=flops, bytes_accessed=1 << 10, transcendentals=1),
+        compiler_params=pltpu.CompilerParams(vmem_limit_bytes=24 << 20),
     )(*args)
 
 
@@ -145,18 +165,27 @@
     owned, width = points.shape
     team = len(TEAMS[0])
     ratio = slab.shape[0] / (owned * lax.axis_size("grp"))
-    other = lax.ppermute(slab, AXES, SWAP)
     copies = jnp.broadcast_to(points[None], (team, owned, width))
     pts = lax.all_to_all(copies, AXES, 0, 0, axis_index_groups=TEAMS).reshape(team * owned, width)
     far = lax.ppermute(pts, AXES, CROSS)
-    sums = (
-        jax.ShapeDtypeStruct((team * owned, width), F32),
-        jax.ShapeDtypeStruct((team * owned, 128), F32),
-    )
-    vec, tot = call(slab_kernel, sums, 1 << 32, pts, slab, other)
+    rows = team * owned
+    half = jax.ShapeDtypeStruct((rows, 256), BF16)
+    wide = jax.ShapeDtypeStruct((rows, 256), F32)
+    narrow = jax.ShapeDtypeStruct((rows, 128), F32)
+
+    held = [pltpu.VMEM((HEAD * TILE, width), F32), pltpu.SemaphoreType.DMA]
+    first = functools.partial(rest_kernel, HEAD)
+    second = functools.partial(rest_kernel, 0)
+    *left, vec, tot = call(head_kernel, (half, half, wide, narrow), COST[0], pts, slab, hbm=(1,), scratch=held)
+    slab_later, _ = lax.optimization_barrier((slab, tot))
+    other = lax.ppermute(slab_later, AXES, SWAP)
+    vec, tot = call(first, (wide, narrow), COST[1], *left, vec, tot, slab)
+    far, _ = lax.optimization_barrier((far, tot))
     far_other = lax.ppermute(far, AXES, SWAP)
+    vec, tot = call(second, (wide, narrow), COST[2], *left, vec, tot, other)
     block = jax.ShapeDtypeStruct((team, owned + 8, width), F32)
-    part = call(functools.partial(pair_kernel, ratio), block, 1 << 28, pts, far, far_other, vec, tot)
+    pair = functools.partial(pair_kernel, ratio)
+    part = call(pair, block, 1 << 28, pts, *left, far, far_other, vec, tot)
     parts = lax.all_to_all(part, AXES, 0, 0, axis_index_groups=TEAMS)
     return call(final_kernel, jax.ShapeDtypeStruct((owned, width), F32), 1 << 16, parts)
 

time: 63.9 us -> 58.8 us (0.920)
  the two profiles are of different devices: /device:TPU:76 before, /device:TPU:74 now
where the time goes in v2:
time: 58.8 us; the launch traced here: 58.4 us
  blocking collectives  44.8 us (76%)
  Pallas kernels  6.33 us (11%)
  starting transfers between devices  5.74 us (10%)
  local copies, waits for them, and re-layouts  0.8 us (1%)
  waiting for transfers between devices  0.74 us (1%)
    all_to_all x1, blocking collectives, shards(): lax.all_to_all(copies, AXES, 0, 0, axis_index_groups=TEAMS)  25.2 us
    all_to_all x1, blocking collectives, shards(): parts = lax.all_to_all(part, AXES, 0, 0, axis_index_groups=TEAMS)  19.6 us
    pallas_call x5, Pallas kernels, call(): pl.pallas_call(kernel, out_shape=shapes, in_specs=[pl.BlockSpec(memory_sp...  6.33 us
    ppermute x1, starting transfers between devices, shards(): other = lax.ppermute(slab_later, AXES, SWAP)  1.92 us
    ppermute x1, starting transfers between devices, shards(): far_other = lax.ppermute(far, AXES, SWAP)  1.91 us
    ppermute x1, starting transfers between devices, shards(): far = lax.ppermute(pts, AXES, CROSS)  1.91 us
  transfers between devices with their start and end apart: 3, of which 1 were waited for; matrix products, arithmetic and copies ran while one was open for 0% of the time, Pallas kernels for 8%

profile of v2, /device:TPU:74, one launch (start us, length us, event | category | flops | bytes accessed | tf_op | source)
XLA Modules:
  0.0 58.4 jit_solution(4257981470532304001)
XLA Ops:
  0.0 0.0 copy-start
  0.0 0.8 %broadcast_in_dim.2 = f32[16,16,128]{2,1,0:T(8,128)S(1)} broadcast(f32[16,128]{1,0:T(8,128)} %param.2), dimensions={1,2} | broadcast | bytes 139264 | tf_op jit(solution)/shard_map/broadcast_in_dim | solution.py:168
  0.8 25.2 %all_to_all.10 = f32[16,16,128]{2,1,0:T(8,128)S(1)} all-to-all(f32[16,16,128]{2,1,0:T(8,128)S(1)} %broadcast_in_dim.2), channel_id=1, replica_groups={{0,4,8,12,16,20,24,28,258,262,266,270,274,278,282,286},{1,5,9,13,17,21,..., dimensions={0} | all-to-all | bytes 262144 | tf_op jit(solution)/shard_map/all_to_all | solution.py:169
  26.0 1.9 %collective-permute-start = (f32[256,128]{1,0:T(8,128)S(1)}, f32[256,128]{1,0:T(8,128)S(1)}, u32[]{:S(2)}, u32[]{:S(2)}) collective-permute-start(f32[256,128]{1,0:T(8,128)S(1)} %bitcast.1), channel_id=1, source_target_pairs={{0,0},{1,1},{2,2},{3,3},{36,4},{37,5},{38,6},{39,7},{72,8},{73,9},... | collective-permute-start | bytes 393224 | tf_op jit(solution)/shard_map/ppermute | solution.py:170
  27.9 1.8 %shard_map.28 = (bf16[256,256]{1,0:T(8,128)(2,1)S(1)}, bf16[256,256]{1,0:T(8,128)(2,1)S(1)}, f32[256,256]{1,0:T(8,128)S(1)}, f32[256,128]{1,0:T(8,128)S(1)}) custom-call(f32[256,128]{1,0:T(8,128)S(1)} %bitcast.2, f32[2048,128]{1,0:T(8,128)} %slab_ref.3), custom_call_target="tpu_custom_call" | custom-call | flops 1048576 | bytes 1024 | tf_op jit(solution)/shard_map/pallas_call | solution.py:153
  29.7 0.0 copy-done
  29.7 1.9 %collective-permute-start.2 = (f32[2048,128]{1,0:T(8,128)S(1)}, f32[2048,128]{1,0:T(8,128)S(1)}, u32[]{:S(2)}, u32[]{:S(2)}) collective-permute-start(f32[2048,128]{1,0:T(8,128)S(1)} %copy-done), channel_id=1, source_target_pairs={{0,1},{1,0},{2,3},{3,2},{4,5},{5,4},{6,7},{7,6},{8,9},{9,8},{10,11... | collective-permute-start | bytes 3145736 | tf_op jit(solution)/shard_map/ppermute | solution.py:181
  31.7 1.4 %shard_map.29 = (f32[256,256]{1,0:T(8,128)S(1)}, f32[256,128]{1,0:T(8,128)S(1)}) custom-call(bf16[256,256]{1,0:T(8,128)(2,1)S(1)} %get-tuple-element.15.left1_ref, bf16[256,256]{1,0:T(8,128)(2,1)S(1)} %get-tuple-element.16.left2_ref, f32[256,256]{1,0:T(8,128)S(1)} %get-tuple-element.17.vec_in, f32[256,128]{1,0:T(8,128)S(1)} %get-tuple-element.18.tot_in, ...), custom_call_target="tpu_custom_call" | custom-call | flops 17179869184 | bytes 1024 | tf_op jit(solution)/shard_map/pallas_call | solution.py:153
  33.0 0.7 %collective-permute-done.first_ref = f32[256,128]{1,0:T(8,128)S(1)} collective-permute-done((f32[256,128]{1,0:T(8,128)S(1)}, f32[256,128]{1,0:T(8,128)S(1)}, u32[]{:S(2)}, u32[]{:S(2)}) %collective-permute-start) | collective-permute-done | bytes 131104 | tf_op jit(solution)/shard_map/ppermute | solution.py:170
  33.8 1.9 %collective-permute-start.1 = (f32[256,128]{1,0:T(8,128)S(1)}, f32[256,128]{1,0:T(8,128)S(1)}, u32[]{:S(2)}, u32[]{:S(2)}) collective-permute-start(f32[256,128]{1,0:T(8,128)S(1)} %collective-permute-done.first_ref), channel_id=1, source_target_pairs={{0,1},{1,0},{2,3},{3,2},{4,5},{5,4},{6,7},{7,6},{8,9},{9,8},{10,11... | collective-permute-start | bytes 393224 | tf_op jit(solution)/shard_map/ppermute | solution.py:184
  35.7 0.0 collective-permute-done.2.slab_ref
  35.7 1.6 %shard_map.30 = (f32[256,256]{1,0:T(8,128)S(1)}, f32[256,128]{1,0:T(8,128)S(1)}) custom-call(bf16[256,256]{1,0:T(8,128)(2,1)S(1)} %get-tuple-element.15.left1_ref, bf16[256,256]{1,0:T(8,128)(2,1)S(1)} %get-tuple-element.16.left2_ref, f32[256,256]{1,0:T(8,128)S(1)} %get-tuple-element.21.vec_in, f32[256,128]{1,0:T(8,128)S(1)} %get-tuple-element.19.tot_in, ...), custom_call_target="tpu_custom_call" | custom-call | flops 2147483648 | bytes 1024 | tf_op jit(solution)/shard_map/pallas_call | solution.py:153
  37.3 0.0 collective-permute-done.1.second_ref
  37.3 0.9 %shard_map.31 = f32[16,24,128]{2,1,0:T(8,128)S(1)} custom-call(f32[256,128]{1,0:T(8,128)S(1)} %bitcast.3, bf16[256,256]{1,0:T(8,128)(2,1)S(1)} %get-tuple-element.15.left1_ref, bf16[256,256]{1,0:T(8,128)(2,1)S(1)} %get-tuple-element.16.left2_ref, f32[256,128]{1,0:T(8,128)S(1)} %collective-permute-done.first_ref, ...), custom_call_target="tpu_custom_call" | custom-call | flops 268435456 | bytes 1024 | tf_op jit(solution)/shard_map/pallas_call | solution.py:153
  38.2 19.6 %all_to_all.11.parts_ref = f32[16,24,128]{2,1,0:T(8,128)S(1)} all-to-all(f32[16,24,128]{2,1,0:T(8,128)S(1)} %shard_map.31), channel_id=1, replica_groups={{0,4,8,12,16,20,24,28,258,262,266,270,274,278,282,286},{1,5,9,13,17,21,..., dimensions={0} | all-to-all | bytes 393216 | tf_op jit(solution)/shard_map/all_to_all | solution.py:189
  57.7 0.7 %shard_map.32 = f32[16,128]{1,0:T(8,128)} custom-call(f32[16,24,128]{2,1,0:T(8,128)S(1)} %all_to_all.11.parts_ref), custom_call_target="tpu_custom_call" | custom-call | flops 65536 | bytes 1024 | tf_op jit(solution)/shard_map/pallas_call | solution.py:153
Async XLA Ops:
  0.0 29.7 %copy-start = (f32[2048,128]{1,0:T(8,128)S(1)}, f32[2048,128]{1,0:T(8,128)}, u32[]{:S(2)}) copy-start(f32[2048,128]{1,0:T(8,128)} %slab_ref.3) | copy-start | bytes 3145732
  26.0 7.7 %collective-permute-start = (f32[256,128]{1,0:T(8,128)S(1)}, f32[256,128]{1,0:T(8,128)S(1)}, u32[]{:S(2)}, u32[]{:S(2)}) collective-permute-start(f32[256,128]{1,0:T(8,128)S(1)} %bitcast.1), channel_id=1, source_target_pairs={{0,0},{1,1},{2,2},{3,3},{36,4},{37,5},{38,6},{39,7},{72,8},{73,9},... | collective-permute-start | bytes 393224 | tf_op jit(solution)/shard_map/ppermute | solution.py:170
  29.7 5.9 %collective-permute-start.2 = (f32[2048,128]{1,0:T(8,128)S(1)}, f32[2048,128]{1,0:T(8,128)S(1)}, u32[]{:S(2)}, u32[]{:S(2)}) collective-permute-start(f32[2048,128]{1,0:T(8,128)S(1)} %copy-done), channel_id=1, source_target_pairs={{0,1},{1,0},{2,3},{3,2},{4,5},{5,4},{6,7},{7,6},{8,9},{9,8},{10,11... | collective-permute-start | bytes 3145736 | tf_op jit(solution)/shard_map/ppermute | solution.py:181
  33.8 3.6 %collective-permute-start.1 = (f32[256,128]{1,0:T(8,128)S(1)}, f32[256,128]{1,0:T(8,128)S(1)}, u32[]{:S(2)}, u32[]{:S(2)}) collective-permute-start(f32[256,128]{1,0:T(8,128)S(1)} %collective-permute-done.first_ref), channel_id=1, source_target_pairs={{0,1},{1,0},{2,3},{3,2},{4,5},{5,4},{6,7},{7,6},{8,9},{9,8},{10,11... | collective-permute-start | bytes 393224 | tf_op jit(solution)/shard_map/ppermute | solution.py:184

commit v3 on v2

--- a/solution.py
+++ b/solution.py
@@ -11,8 +11,7 @@
 AXES = ("grp", "mem")
 CHIPS_X, CHIPS_Y, Z_LO, Z_HI, CORES = 4, 8, 4, 2, 2
 TILE = 512
-HEAD = 1
-COST = (1 << 20, 1 << 34, 1 << 31)
+COST = (1 << 34, 1 << 31)
 
 
 def place(index):
@@ -39,11 +38,13 @@
     TEAMS.setdefault((_x, team_of(_z), _c), []).append(_i)
 TEAMS = list(TEAMS.values())
 
-Z_ORDER = ((0, 2, 1, 3, 4, 6, 5, 7), (1, 0, 3, 2, 6, 7, 4, 5))
+X_ORDER = ((2, 1, 0, 3), (1, 2, 3, 0), (0, 3, 2, 1), (3, 0, 1, 2))
+Z_ORDER = ((0, 2, 1, 3, 4, 6, 5, 7), (1, 3, 0, 2, 5, 7, 4, 6))
 CROSS = []
 for _i in DEVICES:
     _x, _y, _z, _c = place(_i)
-    CROSS.append((index_of((_x + _y) % CHIPS_X, _y, Z_ORDER[_y // CHIPS_X][_z], _c), _i))
+    _far = X_ORDER[_y % CHIPS_X][_x], _y, Z_ORDER[_y // CHIPS_X][_z], _c
+    CROSS.append((index_of(*_far), _i))
 SWAP = [(i, i ^ 1) for i in DEVICES]
 
 
@@ -106,20 +107,27 @@
     return state
 
 
-def head_kernel(pts_ref, slab_ref, left1_ref, left2_ref, vec_ref, tot_ref, held, sem):
-    copy = pltpu.make_async_copy(slab_ref.at[pl.ds(0, held.shape[0])], held, sem)
-    copy.start()
-    pts = pts_ref[...]
-    left = left_operands(pts)
+def own_kernel(pts_ref, slab_ref, left1_ref, left2_ref, vec_ref, tot_ref, held, sems):
+    copies = [
+        pltpu.make_async_copy(slab_ref.at[pl.ds(t * TILE, TILE)], held.at[t], sems.at[t])
+        for t in range(held.shape[0])
+    ]
+    for copy in copies:
+        copy.start()
+    left = left_operands(pts_ref[...])
     left1_ref[...], left2_ref[...] = left
-    copy.wait()
-    vec_ref[...], tot_ref[...] = add_tiles(left, zeros(pts.shape[0]), held, range(HEAD))
-
-
-def rest_kernel(first, left1_ref, left2_ref, vec_in, tot_in, slab_ref, vec_ref, tot_ref):
+    state = zeros(pts_ref.shape[0])
+    for t, copy in enumerate(copies):
+        copy.wait()
+        state = accumulate(left, held[t], state)
+    vec_ref[...], tot_ref[...] = state
+
+
+def other_kernel(left1_ref, left2_ref, vec_in, tot_in, slab_ref, vec_ref, tot_ref):
     left, state = (left1_ref[...], left2_ref[...]), (vec_in[...], tot_in[...])
-    tiles = range(first, slab_ref.shape[0] // TILE)
-    vec_ref[...], tot_ref[...] = add_tiles(left, state, slab_ref, tiles)
+    for t in range(slab_ref.shape[0] // TILE):
+        state = accumulate(left, slab_ref[t * TILE : (t + 1) * TILE, :], state)
+    vec_ref[...], tot_ref[...] = state
 
 
 def pair_kernel(ratio, pts_ref, left1_ref, left2_ref, first_ref, second_ref, vec_ref, tot_ref, out_ref):
@@ -132,19 +140,21 @@
     repel = pts * pair_sum - (state[0][:, :128] + state[0][:, 128:])
     numer = ratio * repel + (vec_ref[:, :128] + vec_ref[:, 128:])
     weight = jnp.sum(tot_ref[...], axis=1, keepdims=True)
-    lane = lax.broadcasted_iota(jnp.int32, (8, 128), 1)
+    spread = jnp.where(lax.broadcasted_iota(jnp.int32, (256, 128), 0) % 16 == lax.broadcasted_iota(jnp.int32, (256, 128), 1), weight, 0.0)
     for k in range(out_ref.shape[0]):
         at = 16 * k
-        out_ref[k, 0:16, :] = numer[at : at + 16]
-        out_ref[k, 16:24, :] = jnp.where(lane < 64, weight[at : at + 8], weight[at + 8 : at + 16])
+        out_ref[k, 0:16, 0, :] = numer[at : at + 16]
+        out_ref[k, 16, 0, :] = jnp.sum(spread[at : at + 16], axis=0)
 
 
 def final_kernel(parts_ref, out_ref):
-    total = parts_ref[0]
+    total = parts_ref[0, :, 0, :]
     for k in range(1, parts_ref.shape[0]):
-        total = total + parts_ref[k]
-    out_ref[0:8, :] = total[0:8] / total[16:24, 0:1]
-    out_ref[8:16, :] = total[8:16] / total[16:24, 127:128]
+        total = total + parts_ref[k, :, 0, :]
+    rows = lax.broadcasted_iota(jnp.int32, (16, 128), 0)
+    lanes = lax.broadcasted_iota(jnp.int32, (16, 128), 1)
+    weight = jnp.sum(jnp.where(rows == lanes, total[16:17], 0.0), axis=1, keepdims=True)
+    out_ref[...] = total[0:16] / weight
 
 
 def call(kernel, shapes, flops, *args, hbm=(), scratch=()):
@@ -173,17 +183,16 @@
     wide = jax.ShapeDtypeStruct((rows, 256), F32)
     narrow = jax.ShapeDtypeStruct((rows, 128), F32)
 
-    held = [pltpu.VMEM((HEAD * TILE, width), F32), pltpu.SemaphoreType.DMA]
-    first = functools.partial(rest_kernel, HEAD)
-    second = functools.partial(rest_kernel, 0)
-    *left, vec, tot = call(head_kernel, (half, half, wide, narrow), COST[0], pts, slab, hbm=(1,), scratch=held)
-    slab_later, _ = lax.optimization_barrier((slab, tot))
+    tiles = slab.shape[0] // TILE
+    held = [pltpu.VMEM((tiles, TILE, width), F32), pltpu.SemaphoreType.DMA((tiles,))]
+    slab_later, _ = lax.optimization_barrier((slab, pts))
     other = lax.ppermute(slab_later, AXES, SWAP)
-    vec, tot = call(first, (wide, narrow), COST[1], *left, vec, tot, slab)
-    far, _ = lax.optimization_barrier((far, tot))
+    own = call(own_kernel, (half, half, wide, narrow), COST[0], pts, slab, hbm=(1,), scratch=held)
+    far, _ = lax.optimization_barrier((far, own[3]))
     far_other = lax.ppermute(far, AXES, SWAP)
-    vec, tot = call(second, (wide, narrow), COST[2], *left, vec, tot, other)
-    block = jax.ShapeDtypeStruct((team, owned + 8, width), F32)
+    left = own[:2]
+    vec, tot = call(other_kernel, (wide, narrow), COST[1], *own, other)
+    block = jax.ShapeDtypeStruct((team, owned + 1, 1, width), F32)
     pair = functools.partial(pair_kernel, ratio)
     part = call(pair, block, 1 << 28, pts, *left, far, far_other, vec, tot)
     parts = lax.all_to_all(part, AXES, 0, 0, axis_index_groups=TEAMS)

time: 58.8 us -> 58.4 us (level)
  the two profiles are of different devices: /device:TPU:74 before, /device:TPU:1 now
where the time goes in v3:
time: 58.4 us; the launch traced here: 57.6 us
  blocking collectives  38.8 us (66%)
  starting transfers between devices  10.9 us (19%)
  Pallas kernels  7.1 us (12%)
  local copies, waits for them, and re-layouts  0.71 us (1%)
    all_to_all x1, blocking collectives, shards(): lax.all_to_all(copies, AXES, 0, 0, axis_index_groups=TEAMS)  25.6 us
    all_to_all x1, blocking collectives, shards(): parts = lax.all_to_all(part, AXES, 0, 0, axis_index_groups=TEAMS)  13.2 us
    pallas_call x4, Pallas kernels, call(): pl.pallas_call(kernel, out_shape=shapes, in_specs=[pl.BlockSpec(memory_sp...  7.1 us
    ppermute x1, starting transfers between devices, shards(): far = lax.ppermute(pts, AXES, CROSS)  4.64 us
    ppermute x1, starting transfers between devices, shards(): other = lax.ppermute(slab_later, AXES, SWAP)  4.3 us
    ppermute x1, starting transfers between devices, shards(): far_other = lax.ppermute(far, AXES, SWAP)  1.92 us
  transfers between devices with their start and end apart: 3, of which 0 were waited for; matrix products, arithmetic and copies ran while one was open for 0% of the time, Pallas kernels for 10%

profile of v3, /device:TPU:1, one launch (start us, length us, event | category | flops | bytes accessed | tf_op | source)
XLA Modules:
  0.0 57.6 jit_solution(11674644193907164053)
XLA Ops:
  0.0 0.7 %broadcast_in_dim.2 = f32[16,16,128]{2,1,0:T(8,128)S(1)} broadcast(f32[16,128]{1,0:T(8,128)} %param.2), dimensions={1,2} | broadcast | bytes 139264 | tf_op jit(solution)/shard_map/broadcast_in_dim | solution.py:178
  0.7 25.6 %all_to_all.10 = f32[16,16,128]{2,1,0:T(8,128)S(1)} all-to-all(f32[16,16,128]{2,1,0:T(8,128)S(1)} %broadcast_in_dim.2), channel_id=1, replica_groups={{0,4,8,12,16,20,24,28,258,262,266,270,274,278,282,286},{1,5,9,13,17,21,..., dimensions={0} | all-to-all | bytes 262144 | tf_op jit(solution)/shard_map/all_to_all | solution.py:179
  26.3 4.6 %collective-permute-start = (f32[256,128]{1,0:T(8,128)S(1)}, f32[256,128]{1,0:T(8,128)S(1)}, u32[]{:S(2)}, u32[]{:S(2)}) collective-permute-start(f32[256,128]{1,0:T(8,128)S(1)} %bitcast.1), channel_id=1, source_target_pairs={{64,0},{65,1},{66,2},{67,3},{36,4},{37,5},{38,6},{39,7},{8,8},{9,9... | collective-permute-start | bytes 393224 | tf_op jit(solution)/shard_map/ppermute | solution.py:180
  31.0 4.3 %collective-permute-start.2 = (f32[2048,128]{1,0:T(8,128)}, f32[2048,128]{1,0:T(8,128)S(1)}, u32[]{:S(2)}, u32[]{:S(2)}) collective-permute-start(f32[2048,128]{1,0:T(8,128)} %slab_ref.1), channel_id=1, source_target_pairs={{0,1},{1,0},{2,3},{3,2},{4,5},{5,4},{6,7},{7,6},{8,9},{9,8},{10,11... | collective-permute-start | bytes 3145736 | tf_op jit(solution)/shard_map/ppermute | solution.py:189
  35.3 3.9 %shard_map.28 = (bf16[256,256]{1,0:T(8,128)(2,1)S(1)}, bf16[256,256]{1,0:T(8,128)(2,1)S(1)}, f32[256,256]{1,0:T(8,128)S(1)}, f32[256,128]{1,0:T(8,128)S(1)}) custom-call(f32[256,128]{1,0:T(8,128)S(1)} %bitcast.2, f32[2048,128]{1,0:T(8,128)} %slab_ref.1), custom_call_target="tpu_custom_call" | custom-call | flops 17179869184 | bytes 1024 | tf_op jit(solution)/shard_map/pallas_call | solution.py:163
  39.2 0.0 collective-permute-done.first_ref
  39.2 1.9 %collective-permute-start.1 = (f32[256,128]{1,0:T(8,128)S(1)}, f32[256,128]{1,0:T(8,128)S(1)}, u32[]{:S(2)}, u32[]{:S(2)}) collective-permute-start(f32[256,128]{1,0:T(8,128)S(1)} %collective-permute-done.first_ref), channel_id=1, source_target_pairs={{0,1},{1,0},{2,3},{3,2},{4,5},{5,4},{6,7},{7,6},{8,9},{9,8},{10,11... | collective-permute-start | bytes 393224 | tf_op jit(solution)/shard_map/ppermute | solution.py:192
  41.1 0.0 collective-permute-done.2.slab_ref
  41.1 1.6 %shard_map.29 = (f32[256,256]{1,0:T(8,128)S(1)}, f32[256,128]{1,0:T(8,128)S(1)}) custom-call(bf16[256,256]{1,0:T(8,128)(2,1)S(1)} %get-tuple-element.13.left1_ref, bf16[256,256]{1,0:T(8,128)(2,1)S(1)} %get-tuple-element.14.left2_ref, f32[256,256]{1,0:T(8,128)S(1)} %get-tuple-element.17.vec_in, f32[256,128]{1,0:T(8,128)S(1)} %get-tuple-element.15.tot_in, ...), custom_call_target="tpu_custom_call" | custom-call | flops 2147483648 | bytes 1024 | tf_op jit(solution)/shard_map/pallas_call | solution.py:163
  42.8 0.0 collective-permute-done.1.second_ref
  42.8 0.9 %shard_map.30 = f32[16,17,1,128]{3,2,1,0:T(1,128)S(1)} custom-call(f32[256,128]{1,0:T(8,128)S(1)} %bitcast.3, bf16[256,256]{1,0:T(8,128)(2,1)S(1)} %get-tuple-element.13.left1_ref, bf16[256,256]{1,0:T(8,128)(2,1)S(1)} %get-tuple-element.14.left2_ref, f32[256,128]{1,0:T(8,128)S(1)} %collective-permute-done.first_ref, ...), custom_call_target="tpu_custom_call" | custom-call | flops 268435456 | bytes 1024 | tf_op jit(solution)/shard_map/pallas_call | solution.py:163
  43.7 13.2 %all_to_all.11.parts_ref = f32[16,17,1,128]{3,2,1,0:T(1,128)S(1)} all-to-all(f32[16,17,1,128]{3,2,1,0:T(1,128)S(1)} %shard_map.30), channel_id=1, replica_groups={{0,4,8,12,16,20,24,28,258,262,266,270,274,278,282,286},{1,5,9,13,17,21,..., dimensions={0} | all-to-all | bytes 278528 | tf_op jit(solution)/shard_map/all_to_all | solution.py:198
  56.9 0.7 %shard_map.31 = f32[16,128]{1,0:T(8,128)} custom-call(f32[16,17,1,128]{3,2,1,0:T(1,128)S(1)} %all_to_all.11.parts_ref), custom_call_target="tpu_custom_call" | custom-call | flops 65536 | bytes 1024 | tf_op jit(solution)/shard_map/pallas_call | solution.py:163
Async XLA Ops:
  26.3 12.8 %collective-permute-start = (f32[256,128]{1,0:T(8,128)S(1)}, f32[256,128]{1,0:T(8,128)S(1)}, u32[]{:S(2)}, u32[]{:S(2)}) collective-permute-start(f32[256,128]{1,0:T(8,128)S(1)} %bitcast.1), channel_id=1, source_target_pairs={{64,0},{65,1},{66,2},{67,3},{36,4},{37,5},{38,6},{39,7},{8,8},{9,9... | collective-permute-start | bytes 393224 | tf_op jit(solution)/shard_map/ppermute | solution.py:180
  31.0 10.1 %collective-permute-start.2 = (f32[2048,128]{1,0:T(8,128)}, f32[2048,128]{1,0:T(8,128)S(1)}, u32[]{:S(2)}, u32[]{:S(2)}) collective-permute-start(f32[2048,128]{1,0:T(8,128)} %slab_ref.1), channel_id=1, source_target_pairs={{0,1},{1,0},{2,3},{3,2},{4,5},{5,4},{6,7},{7,6},{8,9},{9,8},{10,11... | collective-permute-start | bytes 3145736 | tf_op jit(solution)/shard_map/ppermute | solution.py:189
  39.2 3.6 %collective-permute-start.1 = (f32[256,128]{1,0:T(8,128)S(1)}, f32[256,128]{1,0:T(8,128)S(1)}, u32[]{:S(2)}, u32[]{:S(2)}) collective-permute-start(f32[256,128]{1,0:T(8,128)S(1)} %collective-permute-done.first_ref), channel_id=1, source_target_pairs={{0,1},{1,0},{2,3},{3,2},{4,5},{5,4},{6,7},{7,6},{8,9},{9,8},{10,11... | collective-permute-start | bytes 393224 | tf_op jit(solution)/shard_map/ppermute | solution.py:192

commit v4 on v3

--- a/solution.py
+++ b/solution.py
@@ -11,7 +11,7 @@
 AXES = ("grp", "mem")
 CHIPS_X, CHIPS_Y, Z_LO, Z_HI, CORES = 4, 8, 4, 2, 2
 TILE = 512
-COST = (1 << 34, 1 << 31)
+COST = (1 << 20, 1 << 34, 1 << 31)
 
 
 def place(index):
@@ -36,7 +36,14 @@
 for _i in DEVICES:
     _x, _y, _z, _c = place(_i)
     TEAMS.setdefault((_x, team_of(_z), _c), []).append(_i)
-TEAMS = list(TEAMS.values())
+
+
+def rank(index):
+    _, y, z, _ = place(index)
+    return z < Z_LO, (y - 4) % CHIPS_Y
+
+
+TEAMS = [sorted(team, key=rank) for team in TEAMS.values()]
 
 X_ORDER = ((2, 1, 0, 3), (1, 2, 3, 0), (0, 3, 2, 1), (3, 0, 1, 2))
 Z_ORDER = ((0, 2, 1, 3, 4, 6, 5, 7), (1, 3, 0, 2, 5, 7, 4, 6))
@@ -107,27 +114,21 @@
     return state
 
 
-def own_kernel(pts_ref, slab_ref, left1_ref, left2_ref, vec_ref, tot_ref, held, sems):
-    copies = [
-        pltpu.make_async_copy(slab_ref.at[pl.ds(t * TILE, TILE)], held.at[t], sems.at[t])
-        for t in range(held.shape[0])
-    ]
-    for copy in copies:
-        copy.start()
-    left = left_operands(pts_ref[...])
-    left1_ref[...], left2_ref[...] = left
-    state = zeros(pts_ref.shape[0])
-    for t, copy in enumerate(copies):
-        copy.wait()
-        state = accumulate(left, held[t], state)
-    vec_ref[...], tot_ref[...] = state
+def left_kernel(pts_ref, slab_ref, left1_ref, left2_ref):
+    del slab_ref
+    left1_ref[...], left2_ref[...] = left_operands(pts_ref[...])
+
+
+def own_kernel(left1_ref, left2_ref, slab_ref, vec_ref, tot_ref):
+    left = left1_ref[...], left2_ref[...]
+    tiles = range(slab_ref.shape[0] // TILE)
+    vec_ref[...], tot_ref[...] = add_tiles(left, zeros(left[0].shape[0]), slab_ref, tiles)
 
 
 def other_kernel(left1_ref, left2_ref, vec_in, tot_in, slab_ref, vec_ref, tot_ref):
     left, state = (left1_ref[...], left2_ref[...]), (vec_in[...], tot_in[...])
-    for t in range(slab_ref.shape[0] // TILE):
-        state = accumulate(left, slab_ref[t * TILE : (t + 1) * TILE, :], state)
-    vec_ref[...], tot_ref[...] = state
+    tiles = range(slab_ref.shape[0] // TILE)
+    vec_ref[...], tot_ref[...] = add_tiles(left, state, slab_ref, tiles)
 
 
 def pair_kernel(ratio, pts_ref, left1_ref, left2_ref, first_ref, second_ref, vec_ref, tot_ref, out_ref):
@@ -157,7 +158,7 @@
     out_ref[...] = total[0:16] / weight
 
 
-def call(kernel, shapes, flops, *args, hbm=(), scratch=()):
+def call(kernel, shapes, flops, *args, hbm=()):
     args = [pltpu.with_memory_space_constraint(a, pltpu.HBM) if k in hbm else a for k, a in enumerate(args)]
     spaces = [pltpu.HBM if k in hbm else pltpu.VMEM for k in range(len(args))]
     return pl.pallas_call(
@@ -165,7 +166,6 @@
         out_shape=shapes,
         in_specs=[pl.BlockSpec(memory_space=space) for space in spaces],
         out_specs=jax.tree.map(lambda _: pl.BlockSpec(memory_space=pltpu.VMEM), shapes),
-        scratch_shapes=scratch,
         cost_estimate=pl.CostEstimate(flops=flops, bytes_accessed=1 << 10, transcendentals=1),
         compiler_params=pltpu.CompilerParams(vmem_limit_bytes=24 << 20),
     )(*args)
@@ -183,15 +183,13 @@
     wide = jax.ShapeDtypeStruct((rows, 256), F32)
     narrow = jax.ShapeDtypeStruct((rows, 128), F32)
 
-    tiles = slab.shape[0] // TILE
-    held = [pltpu.VMEM((tiles, TILE, width), F32), pltpu.SemaphoreType.DMA((tiles,))]
-    slab_later, _ = lax.optimization_barrier((slab, pts))
+    left = call(left_kernel, (half, half), COST[0], pts, slab, hbm=(1,))
+    slab_later, _ = lax.optimization_barrier((slab, left[0]))
     other = lax.ppermute(slab_later, AXES, SWAP)
-    own = call(own_kernel, (half, half, wide, narrow), COST[0], pts, slab, hbm=(1,), scratch=held)
-    far, _ = lax.optimization_barrier((far, own[3]))
+    vec, tot = call(own_kernel, (wide, narrow), COST[1], *left, slab)
+    far, _ = lax.optimization_barrier((far, tot))
     far_other = lax.ppermute(far, AXES, SWAP)
-    left = own[:2]
-    vec, tot = call(other_kernel, (wide, narrow), COST[1], *own, other)
+    vec, tot = call(other_kernel, (wide, narrow), COST[2], *left, vec, tot, other)
     block = jax.ShapeDtypeStruct((team, owned + 1, 1, width), F32)
     pair = functools.partial(pair_kernel, ratio)
     part = call(pair, block, 1 << 28, pts, *left, far, far_other, vec, tot)

time: 58.4 us -> 52.4 us (0.90); the launches traced: 57.6 us -> 52.2 us
  Pallas kernels: 7.1 us -> 4.97 us
  blocking collectives: 38.8 us -> 36.7 us
  starting transfers between devices: 10.9 us -> 9.63 us
    all_to_all x1, blocking collectives: 25.6 us -> 21.4 us  [shards(): lax.all_to_all(copies, AXES, 0, 0, axis_index_groups=TEAMS)]
    pallas_call x4 -> x5, Pallas kernels: 7.1 us -> 4.97 us  [call(): pl.pallas_call(kernel, out_shape=shapes, in_specs=[pl.BlockSpec(memory_sp...]
    all_to_all x1, blocking collectives: 13.2 us -> 15.3 us  [shards(): parts = lax.all_to_all(part, AXES, 0, 0, axis_index_groups=TEAMS)]
    ppermute x1, starting transfers between devices: 4.3 us -> 3.07 us  [shards(): other = lax.ppermute(slab_later, AXES, SWAP)]
  transfers between devices with their start and end apart: 3 -> 3, of which waited for: 0 -> 0; matrix products, arithmetic and copies ran while one was open for 0% -> 0% of each run, Pallas kernels for 10% -> 6%
where the time goes in v4:
time: 52.4 us; the launch traced here: 52.2 us
  blocking collectives  36.7 us (70%)
  starting transfers between devices  9.63 us (18%)
  Pallas kernels  4.97 us (9%)
  local copies, waits for them, and re-layouts  0.8 us (2%)
    all_to_all x1, blocking collectives, shards(): lax.all_to_all(copies, AXES, 0, 0, axis_index_groups=TEAMS)  21.4 us
    all_to_all x1, blocking collectives, shards(): parts = lax.all_to_all(part, AXES, 0, 0, axis_index_groups=TEAMS)  15.3 us
    pallas_call x5, Pallas kernels, call(): pl.pallas_call(kernel, out_shape=shapes, in_specs=[pl.BlockSpec(memory_sp...  4.97 us
    ppermute x1, starting transfers between devices, shards(): far = lax.ppermute(pts, AXES, CROSS)  4.64 us
    ppermute x1, starting transfers between devices, shards(): other = lax.ppermute(slab_later, AXES, SWAP)  3.07 us
    ppermute x1, starting transfers between devices, shards(): far_other = lax.ppermute(far, AXES, SWAP)  1.92 us
  transfers between devices with their start and end apart: 3, of which 0 were waited for; matrix products, arithmetic and copies ran while one was open for 0% of the time, Pallas kernels for 6%

profile of v4, /device:TPU:1, one launch (start us, length us, event | category | flops | bytes accessed | tf_op | source)
XLA Modules:
  0.0 52.2 jit_solution(1349034601734041001)
XLA Ops:
  0.0 0.0 copy-start
  0.0 0.8 %broadcast_in_dim.2 = f32[16,16,128]{2,1,0:T(8,128)S(1)} broadcast(f32[16,128]{1,0:T(8,128)} %param.2), dimensions={1,2} | broadcast | bytes 139264 | tf_op jit(solution)/shard_map/broadcast_in_dim | solution.py:178
  0.8 21.4 %all_to_all.10 = f32[16,16,128]{2,1,0:T(8,128)S(1)} all-to-all(f32[16,16,128]{2,1,0:T(8,128)S(1)} %broadcast_in_dim.2), channel_id=1, replica_groups={{274,278,282,286,258,262,266,270,16,20,24,28,0,4,8,12},{275,279,283,287..., dimensions={0} | all-to-all | bytes 262144 | tf_op jit(solution)/shard_map/all_to_all | solution.py:179
  22.2 4.6 %collective-permute-start = (f32[256,128]{1,0:T(8,128)S(1)}, f32[256,128]{1,0:T(8,128)S(1)}, u32[]{:S(2)}, u32[]{:S(2)}) collective-permute-start(f32[256,128]{1,0:T(8,128)S(1)} %bitcast.1), channel_id=1, source_target_pairs={{64,0},{65,1},{66,2},{67,3},{36,4},{37,5},{38,6},{39,7},{8,8},{9,9... | collective-permute-start | bytes 393224 | tf_op jit(solution)/shard_map/ppermute | solution.py:180
  26.8 0.1 shard_map.28
  27.0 0.0 copy-done
  27.0 3.1 %collective-permute-start.2 = (f32[2048,128]{1,0:T(8,128)S(1)}, f32[2048,128]{1,0:T(8,128)S(1)}, u32[]{:S(2)}, u32[]{:S(2)}) collective-permute-start(f32[2048,128]{1,0:T(8,128)S(1)} %copy-done), channel_id=1, source_target_pairs={{0,1},{1,0},{2,3},{3,2},{4,5},{5,4},{6,7},{7,6},{8,9},{9,8},{10,11... | collective-permute-start | bytes 3145736 | tf_op jit(solution)/shard_map/ppermute | solution.py:188
  30.0 1.6 %shard_map.29 = (f32[256,256]{1,0:T(8,128)S(1)}, f32[256,128]{1,0:T(8,128)S(1)}) custom-call(bf16[256,256]{1,0:T(8,128)(2,1)S(1)} %get-tuple-element.13.left1_ref, bf16[256,256]{1,0:T(8,128)(2,1)S(1)} %get-tuple-element.14.left2_ref, f32[2048,128]{1,0:T(8,128)S(1)} %copy-done), custom_call_target="tpu_custom_call" | custom-call | flops 17179869184 | bytes 1024 | tf_op jit(solution)/shard_map/pallas_call | solution.py:164
  31.7 0.0 collective-permute-done.first_ref
  31.7 1.9 %collective-permute-start.1 = (f32[256,128]{1,0:T(8,128)S(1)}, f32[256,128]{1,0:T(8,128)S(1)}, u32[]{:S(2)}, u32[]{:S(2)}) collective-permute-start(f32[256,128]{1,0:T(8,128)S(1)} %collective-permute-done.first_ref), channel_id=1, source_target_pairs={{0,1},{1,0},{2,3},{3,2},{4,5},{5,4},{6,7},{7,6},{8,9},{9,8},{10,11... | collective-permute-start | bytes 393224 | tf_op jit(solution)/shard_map/ppermute | solution.py:191
  33.6 0.0 collective-permute-done.2.slab_ref
  33.6 1.6 %shard_map.30 = (f32[256,256]{1,0:T(8,128)S(1)}, f32[256,128]{1,0:T(8,128)S(1)}) custom-call(bf16[256,256]{1,0:T(8,128)(2,1)S(1)} %get-tuple-element.13.left1_ref, bf16[256,256]{1,0:T(8,128)(2,1)S(1)} %get-tuple-element.14.left2_ref, f32[256,256]{1,0:T(8,128)S(1)} %get-tuple-element.17.vec_in, f32[256,128]{1,0:T(8,128)S(1)} %get-tuple-element.15.tot_in, ...), custom_call_target="tpu_custom_call" | custom-call | flops 2147483648 | bytes 1024 | tf_op jit(solution)/shard_map/pallas_call | solution.py:164
  35.3 0.0 collective-permute-done.1.second_ref
  35.3 0.9 %shard_map.31 = f32[16,17,1,128]{3,2,1,0:T(1,128)S(1)} custom-call(f32[256,128]{1,0:T(8,128)S(1)} %bitcast.3, bf16[256,256]{1,0:T(8,128)(2,1)S(1)} %get-tuple-element.13.left1_ref, bf16[256,256]{1,0:T(8,128)(2,1)S(1)} %get-tuple-element.14.left2_ref, f32[256,128]{1,0:T(8,128)S(1)} %collective-permute-done.first_ref, ...), custom_call_target="tpu_custom_call" | custom-call | flops 268435456 | bytes 1024 | tf_op jit(solution)/shard_map/pallas_call | solution.py:164
  36.2 15.3 %all_to_all.11.parts_ref = f32[16,17,1,128]{3,2,1,0:T(1,128)S(1)} all-to-all(f32[16,17,1,128]{3,2,1,0:T(1,128)S(1)} %shard_map.31), channel_id=1, replica_groups={{274,278,282,286,258,262,266,270,16,20,24,28,0,4,8,12},{275,279,283,287..., dimensions={0} | all-to-all | bytes 278528 | tf_op jit(solution)/shard_map/all_to_all | solution.py:196
  51.5 0.7 %shard_map.32 = f32[16,128]{1,0:T(8,128)} custom-call(f32[16,17,1,128]{3,2,1,0:T(1,128)S(1)} %all_to_all.11.parts_ref), custom_call_target="tpu_custom_call" | custom-call | flops 65536 | bytes 1024 | tf_op jit(solution)/shard_map/pallas_call | solution.py:164
Async XLA Ops:
  0.0 27.0 %copy-start = (f32[2048,128]{1,0:T(8,128)S(1)}, f32[2048,128]{1,0:T(8,128)}, u32[]{:S(2)}) copy-start(f32[2048,128]{1,0:T(8,128)} %slab_ref.3) | copy-start | bytes 3145732
  22.2 9.5 %collective-permute-start = (f32[256,128]{1,0:T(8,128)S(1)}, f32[256,128]{1,0:T(8,128)S(1)}, u32[]{:S(2)}, u32[]{:S(2)}) collective-permute-start(f32[256,128]{1,0:T(8,128)S(1)} %bitcast.1), channel_id=1, source_target_pairs={{64,0},{65,1},{66,2},{67,3},{36,4},{37,5},{38,6},{39,7},{8,8},{9,9... | collective-permute-start | bytes 393224 | tf_op jit(solution)/shard_map/ppermute | solution.py:180
  27.0 6.7 %collective-permute-start.2 = (f32[2048,128]{1,0:T(8,128)S(1)}, f32[2048,128]{1,0:T(8,128)S(1)}, u32[]{:S(2)}, u32[]{:S(2)}) collective-permute-start(f32[2048,128]{1,0:T(8,128)S(1)} %copy-done), channel_id=1, source_target_pairs={{0,1},{1,0},{2,3},{3,2},{4,5},{5,4},{6,7},{7,6},{8,9},{9,8},{10,11... | collective-permute-start | bytes 3145736 | tf_op jit(solution)/shard_map/ppermute | solution.py:188
  31.7 3.6 %collective-permute-start.1 = (f32[256,128]{1,0:T(8,128)S(1)}, f32[256,128]{1,0:T(8,128)S(1)}, u32[]{:S(2)}, u32[]{:S(2)}) collective-permute-start(f32[256,128]{1,0:T(8,128)S(1)} %collective-permute-done.first_ref), channel_id=1, source_target_pairs={{0,1},{1,0},{2,3},{3,2},{4,5},{5,4},{6,7},{7,6},{8,9},{9,8},{10,11... | collective-permute-start | bytes 393224 | tf_op jit(solution)/shard_map/ppermute | solution.py:191

commit v5 on v4

--- a/solution.py
+++ b/solution.py
@@ -10,7 +10,6 @@
 F32, BF16 = jnp.float32, jnp.bfloat16
 AXES = ("grp", "mem")
 CHIPS_X, CHIPS_Y, Z_LO, Z_HI, CORES = 4, 8, 4, 2, 2
-TILE = 512
 COST = (1 << 20, 1 << 34, 1 << 31)
 
 
@@ -45,13 +44,21 @@
 
 TEAMS = [sorted(team, key=rank) for team in TEAMS.values()]
 
-X_ORDER = ((2, 1, 0, 3), (1, 2, 3, 0), (0, 3, 2, 1), (3, 0, 1, 2))
-Z_ORDER = ((0, 2, 1, 3, 4, 6, 5, 7), (1, 3, 0, 2, 5, 7, 4, 6))
-CROSS = []
-for _i in DEVICES:
-    _x, _y, _z, _c = place(_i)
-    _far = X_ORDER[_y % CHIPS_X][_x], _y, Z_ORDER[_y // CHIPS_X][_z], _c
-    CROSS.append((index_of(*_far), _i))
+X_FAR = ((2, 1, 0, 3), (1, 2, 3, 0), (0, 3, 2, 1), (3, 0, 1, 2))
+X_NEAR = ((3, 0, 1, 2), (0, 3, 2, 1), (1, 2, 3, 0), (2, 1, 0, 3))
+Z_FAR, Z_NEAR = (1, 3, 0, 2, 5, 7, 4, 6), (0, 2, 1, 3, 4, 6, 5, 7)
+
+
+def cross(x_orders, z_order):
+    pairs = []
+    for i in DEVICES:
+        x, y, z, core = place(i)
+        flip, step = divmod(y, CHIPS_X)
+        pairs.append((index_of(x_orders[step][x], y, z_order[z], core ^ flip), i))
+    return pairs
+
+
+FAR, NEAR = cross(X_FAR, Z_FAR), cross(X_NEAR, Z_NEAR)
 SWAP = [(i, i ^ 1) for i in DEVICES]
 
 
@@ -86,8 +93,7 @@
     return jnp.concatenate([hi, hi], axis=1), jnp.concatenate([lo, columns(None, norm)], axis=1)
 
 
-def accumulate(left, rows, state):
-    vec, tot = state
+def sums_of(left, rows):
     hi, lo = split2(rows)
     norm = jnp.sum(rows * rows, axis=1, keepdims=True)
     both = jnp.concatenate([hi, lo], axis=1)
@@ -96,22 +102,16 @@
     d = d + lax.dot_general(left[1], extra, NT, preferred_element_type=F32)
     w = lax.rsqrt(jnp.maximum(d, 1.0))
     w_hi, w_lo = split2(w)
-    part = jnp.dot(w_hi, both, preferred_element_type=F32)
-    part = part + jnp.dot(w_lo, both, preferred_element_type=F32)
-    vec = vec + part
-    for k in range(rows.shape[0] // 128):
-        tot = tot + w[:, 128 * k : 128 * (k + 1)]
-    return vec, tot
-
-
-def zeros(rows):
-    return jnp.zeros((rows, 256), F32), jnp.zeros((rows, 128), F32)
-
-
-def add_tiles(left, state, slab_ref, tiles):
-    for t in tiles:
-        state = accumulate(left, slab_ref[t * TILE : (t + 1) * TILE, :], state)
-    return state
+    count = w.shape[0]
+    vec = jnp.zeros((count, both.shape[1]), F32)
+    for at in range(0, rows.shape[0], 256):
+        part = jnp.concatenate([w_hi[:, at : at + 256], w_lo[:, at : at + 256]], axis=0)
+        part = jnp.dot(part, both[at : at + 256], preferred_element_type=F32)
+        vec = vec + (part[:count] + part[count:])
+    tot = w[:, 0:128]
+    for at in range(128, rows.shape[0], 128):
+        tot = tot + w[:, at : at + 128]
+    return vec[:, :128] + vec[:, 128:], tot
 
 
 def left_kernel(pts_ref, slab_ref, left1_ref, left2_ref):
@@ -119,29 +119,20 @@
     left1_ref[...], left2_ref[...] = left_operands(pts_ref[...])
 
 
-def own_kernel(left1_ref, left2_ref, slab_ref, vec_ref, tot_ref):
-    left = left1_ref[...], left2_ref[...]
-    tiles = range(slab_ref.shape[0] // TILE)
-    vec_ref[...], tot_ref[...] = add_tiles(left, zeros(left[0].shape[0]), slab_ref, tiles)
+def sums_kernel(left1_ref, left2_ref, rows_ref, vec_ref, tot_ref):
+    vec_ref[...], tot_ref[...] = sums_of((left1_ref[...], left2_ref[...]), rows_ref[...])
 
 
-def other_kernel(left1_ref, left2_ref, vec_in, tot_in, slab_ref, vec_ref, tot_ref):
-    left, state = (left1_ref[...], left2_ref[...]), (vec_in[...], tot_in[...])
-    tiles = range(slab_ref.shape[0] // TILE)
-    vec_ref[...], tot_ref[...] = add_tiles(left, state, slab_ref, tiles)
-
-
-def pair_kernel(ratio, pts_ref, left1_ref, left2_ref, first_ref, second_ref, vec_ref, tot_ref, out_ref):
-    pts = pts_ref[...]
-    left = left1_ref[...], left2_ref[...]
-    state = zeros(pts.shape[0])
-    for ref in (first_ref, second_ref):
-        state = accumulate(left, ref[...], state)
-    pair_sum = jnp.sum(state[1], axis=1, keepdims=True)
-    repel = pts * pair_sum - (state[0][:, :128] + state[0][:, 128:])
-    numer = ratio * repel + (vec_ref[:, :128] + vec_ref[:, 128:])
-    weight = jnp.sum(tot_ref[...], axis=1, keepdims=True)
-    spread = jnp.where(lax.broadcasted_iota(jnp.int32, (256, 128), 0) % 16 == lax.broadcasted_iota(jnp.int32, (256, 128), 1), weight, 0.0)
+def last_kernel(ratio, pts_ref, left1_ref, left2_ref, rows_ref, *refs):
+    *sums, out_ref = refs
+    own_vec, own_tot, other_vec, other_tot, far_vec, far_tot = (ref[...] for ref in sums)
+    near_vec, near_tot = sums_of((left1_ref[...], left2_ref[...]), rows_ref[...])
+    pair_sum = jnp.sum(far_tot + near_tot, axis=1, keepdims=True)
+    repel = pts_ref[...] * pair_sum - (far_vec + near_vec)
+    numer = ratio * repel + (own_vec + other_vec)
+    weight = jnp.sum(own_tot + other_tot, axis=1, keepdims=True)
+    points, lanes = (lax.broadcasted_iota(jnp.int32, numer.shape, k) for k in (0, 1))
+    spread = jnp.where(points % 16 == lanes, weight, 0.0)
     for k in range(out_ref.shape[0]):
         at = 16 * k
         out_ref[k, 0:16, 0, :] = numer[at : at + 16]
@@ -177,22 +168,23 @@
     ratio = slab.shape[0] / (owned * lax.axis_size("grp"))
     copies = jnp.broadcast_to(points[None], (team, owned, width))
     pts = lax.all_to_all(copies, AXES, 0, 0, axis_index_groups=TEAMS).reshape(team * owned, width)
-    far = lax.ppermute(pts, AXES, CROSS)
+    far = lax.ppermute(pts, AXES, FAR)
+    near = lax.ppermute(pts, AXES, NEAR)
     rows = team * owned
     half = jax.ShapeDtypeStruct((rows, 256), BF16)
-    wide = jax.ShapeDtypeStruct((rows, 256), F32)
-    narrow = jax.ShapeDtypeStruct((rows, 128), F32)
+    whole = jax.ShapeDtypeStruct((rows, width), F32)
 
     left = call(left_kernel, (half, half), COST[0], pts, slab, hbm=(1,))
     slab_later, _ = lax.optimization_barrier((slab, left[0]))
     other = lax.ppermute(slab_later, AXES, SWAP)
-    vec, tot = call(own_kernel, (wide, narrow), COST[1], *left, slab)
-    far, _ = lax.optimization_barrier((far, tot))
-    far_other = lax.ppermute(far, AXES, SWAP)
-    vec, tot = call(other_kernel, (wide, narrow), COST[2], *left, vec, tot, other)
+    own_sums = call(sums_kernel, (whole, whole), COST[1], *left, slab)
+    far, _ = lax.optimization_barrier((far, own_sums[1]))
+    far_sums = call(sums_kernel, (whole, whole), COST[2], *left, far)
+    other, *far_sums = lax.optimization_barrier((other, *far_sums))
+    other_sums = call(sums_kernel, (whole, whole), COST[2], *left, other)
+    last = functools.partial(last_kernel, ratio)
     block = jax.ShapeDtypeStruct((team, owned + 1, 1, width), F32)
-    pair = functools.partial(pair_kernel, ratio)
-    part = call(pair, block, 1 << 28, pts, *left, far, far_other, vec, tot)
+    part = call(last, block, 1 << 28, pts, *left, near, *own_sums, *other_sums, *far_sums)
     parts = lax.all_to_all(part, AXES, 0, 0, axis_index_groups=TEAMS)
     return call(final_kernel, jax.ShapeDtypeStruct((owned, width), F32), 1 << 16, parts)
 

time: 52.4 us -> 51.6 us (0.985)
  blocking collectives: 36.7 us -> 35.4 us
    all_to_all x1, blocking collectives: 15.3 us -> 14 us  [shards(): parts = lax.all_to_all(part, AXES, 0, 0, axis_index_groups=TEAMS)]
    pallas_call x5 -> x6, Pallas kernels: 4.97 us -> 5.01 us  [call(): pl.pallas_call(kernel, out_shape=shapes, in_specs=[pl.BlockSpec(memory_sp...]
  transfers between devices with their start and end apart: 3 -> 3, of which waited for: 0 -> 1; matrix products, arithmetic and copies ran while one was open for 0% -> 0% of each run, Pallas kernels for 6% -> 7%
where the time goes in v5:
time: 51.6 us; the launch traced here: 51.3 us
  blocking collectives  35.4 us (69%)
  starting transfers between devices  9.79 us (19%)
  Pallas kernels  5.01 us (10%)
  local copies, waits for them, and re-layouts  0.8 us (2%)
    all_to_all x1, blocking collectives, shards(): lax.all_to_all(copies, AXES, 0, 0, axis_index_groups=TEAMS)  21.4 us
    all_to_all x1, blocking collectives, shards(): parts = lax.all_to_all(part, AXES, 0, 0, axis_index_groups=TEAMS)  14 us
    pallas_call x6, Pallas kernels, call(): pl.pallas_call(kernel, out_shape=shapes, in_specs=[pl.BlockSpec(memory_sp...  5.01 us
    ppermute x1, starting transfers between devices, shards(): far = lax.ppermute(pts, AXES, FAR)  4.62 us
    ppermute x1, starting transfers between devices, shards(): other = lax.ppermute(slab_later, AXES, SWAP)  3.25 us
    ppermute x1, starting transfers between devices, shards(): near = lax.ppermute(pts, AXES, NEAR)  1.92 us
  transfers between devices with their start and end apart: 3, of which 1 were waited for; matrix products, arithmetic and copies ran while one was open for 0% of the time, Pallas kernels for 7%

profile of v5, /device:TPU:1, one launch (start us, length us, event | category | flops | bytes accessed | tf_op | source)
XLA Modules:
  0.0 51.3 jit_solution(10920107928477773337)
XLA Ops:
  0.0 0.0 copy-start
  0.0 0.8 %broadcast_in_dim.2 = f32[16,16,128]{2,1,0:T(8,128)S(1)} broadcast(f32[16,128]{1,0:T(8,128)} %param.2), dimensions={1,2} | broadcast | bytes 139264 | tf_op jit(solution)/shard_map/broadcast_in_dim | solution.py:169
  0.8 21.4 %all_to_all.10 = f32[16,16,128]{2,1,0:T(8,128)S(1)} all-to-all(f32[16,16,128]{2,1,0:T(8,128)S(1)} %broadcast_in_dim.2), channel_id=1, replica_groups={{274,278,282,286,258,262,266,270,16,20,24,28,0,4,8,12},{275,279,283,287..., dimensions={0} | all-to-all | bytes 262144 | tf_op jit(solution)/shard_map/all_to_all | solution.py:170
  22.2 4.6 %collective-permute-start.2 = (f32[256,128]{1,0:T(8,128)S(1)}, f32[256,128]{1,0:T(8,128)S(1)}, u32[]{:S(2)}, u32[]{:S(2)}) collective-permute-start(f32[256,128]{1,0:T(8,128)S(1)} %bitcast.1), channel_id=1, source_target_pairs={{192,0},{193,1},{194,2},{195,3},{164,4},{165,5},{166,6},{167,7},{1... | collective-permute-start | bytes 393224 | tf_op jit(solution)/shard_map/ppermute | solution.py:171
  26.8 1.9 %collective-permute-start = (f32[256,128]{1,0:T(8,128)S(1)}, f32[256,128]{1,0:T(8,128)S(1)}, u32[]{:S(2)}, u32[]{:S(2)}) collective-permute-start(f32[256,128]{1,0:T(8,128)S(1)} %bitcast.2), channel_id=1, source_target_pairs={{96,0},{97,1},{98,2},{99,3},{4,4},{5,5},{6,6},{7,7},{40,8},{41,9},... | collective-permute-start | bytes 393224 | tf_op jit(solution)/shard_map/ppermute | solution.py:172
  28.7 0.1 shard_map.28
  28.9 0.0 copy-done
  28.9 3.2 %collective-permute-start.1 = (f32[2048,128]{1,0:T(8,128)S(1)}, f32[2048,128]{1,0:T(8,128)S(1)}, u32[]{:S(2)}, u32[]{:S(2)}) collective-permute-start(f32[2048,128]{1,0:T(8,128)S(1)} %copy-done), channel_id=1, source_target_pairs={{0,1},{1,0},{2,3},{3,2},{4,5},{5,4},{6,7},{7,6},{8,9},{9,8},{10,11... | collective-permute-start | bytes 3145736 | tf_op jit(solution)/shard_map/ppermute | solution.py:179
  32.1 1.5 %shard_map.29 = (f32[256,128]{1,0:T(8,128)S(1)}, f32[256,128]{1,0:T(8,128)S(1)}) custom-call(bf16[256,256]{1,0:T(8,128)(2,1)S(1)} %get-tuple-element.18.left1_ref, bf16[256,256]{1,0:T(8,128)(2,1)S(1)} %get-tuple-element.19.left2_ref, f32[2048,128]{1,0:T(8,128)S(1)} %copy-done), custom_call_target="tpu_custom_call" | custom-call | flops 17179869184 | bytes 1024 | tf_op jit(solution)/shard_map/pallas_call | solution.py:155
  33.6 0.0 collective-permute-done.2.rows_ref
  33.6 0.6 %shard_map.30 = (f32[256,128]{1,0:T(8,128)S(1)}, f32[256,128]{1,0:T(8,128)S(1)}) custom-call(bf16[256,256]{1,0:T(8,128)(2,1)S(1)} %get-tuple-element.18.left1_ref, bf16[256,256]{1,0:T(8,128)(2,1)S(1)} %get-tuple-element.19.left2_ref, f32[256,128]{1,0:T(8,128)S(1)} %collective-permute-done.2.rows_ref), custom_call_target="tpu_custom_call" | custom-call | flops 2147483648 | bytes 1024 | tf_op jit(solution)/shard_map/pallas_call | solution.py:155
  34.2 0.2 collective-permute-done.1.rows_ref
  34.4 1.5 %shard_map.31 = (f32[256,128]{1,0:T(8,128)S(1)}, f32[256,128]{1,0:T(8,128)S(1)}) custom-call(bf16[256,256]{1,0:T(8,128)(2,1)S(1)} %get-tuple-element.18.left1_ref, bf16[256,256]{1,0:T(8,128)(2,1)S(1)} %get-tuple-element.19.left2_ref, f32[2048,128]{1,0:T(8,128)S(1)} %collective-permute-done.1.rows_ref), custom_call_target="tpu_custom_call" | custom-call | flops 2147483648 | bytes 1024 | tf_op jit(solution)/shard_map/pallas_call | solution.py:155
  35.9 0.0 collective-permute-done.rows_ref
  35.9 0.6 %shard_map.32 = f32[16,17,1,128]{3,2,1,0:T(1,128)S(1)} custom-call(f32[256,128]{1,0:T(8,128)S(1)} %bitcast.4, bf16[256,256]{1,0:T(8,128)(2,1)S(1)} %get-tuple-element.18.left1_ref, bf16[256,256]{1,0:T(8,128)(2,1)S(1)} %get-tuple-element.19.left2_ref, f32[256,128]{1,0:T(8,128)S(1)} %collective-permute-done.rows_ref, ...), custom_call_target="tpu_custom_call" | custom-call | flops 268435456 | bytes 1024 | tf_op jit(solution)/shard_map/pallas_call | solution.py:155
  36.5 14.0 %all_to_all.11.parts_ref = f32[16,17,1,128]{3,2,1,0:T(1,128)S(1)} all-to-all(f32[16,17,1,128]{3,2,1,0:T(1,128)S(1)} %shard_map.32), channel_id=1, replica_groups={{274,278,282,286,258,262,266,270,16,20,24,28,0,4,8,12},{275,279,283,287..., dimensions={0} | all-to-all | bytes 278528 | tf_op jit(solution)/shard_map/all_to_all | solution.py:188
  50.6 0.7 %shard_map.33 = f32[16,128]{1,0:T(8,128)} custom-call(f32[16,17,1,128]{3,2,1,0:T(1,128)S(1)} %all_to_all.11.parts_ref), custom_call_target="tpu_custom_call" | custom-call | flops 65536 | bytes 1024 | tf_op jit(solution)/shard_map/pallas_call | solution.py:155
Async XLA Ops:
  0.0 28.9 %copy-start = (f32[2048,128]{1,0:T(8,128)S(1)}, f32[2048,128]{1,0:T(8,128)}, u32[]{:S(2)}) copy-start(f32[2048,128]{1,0:T(8,128)} %rows_ref.1) | copy-start | bytes 3145732
  22.2 11.4 %collective-permute-start.2 = (f32[256,128]{1,0:T(8,128)S(1)}, f32[256,128]{1,0:T(8,128)S(1)}, u32[]{:S(2)}, u32[]{:S(2)}) collective-permute-start(f32[256,128]{1,0:T(8,128)S(1)} %bitcast.1), channel_id=1, source_target_pairs={{192,0},{193,1},{194,2},{195,3},{164,4},{165,5},{166,6},{167,7},{1... | collective-permute-start | bytes 393224 | tf_op jit(solution)/shard_map/ppermute | solution.py:171
  26.8 9.1 %collective-permute-start = (f32[256,128]{1,0:T(8,128)S(1)}, f32[256,128]{1,0:T(8,128)S(1)}, u32[]{:S(2)}, u32[]{:S(2)}) collective-permute-start(f32[256,128]{1,0:T(8,128)S(1)} %bitcast.2), channel_id=1, source_target_pairs={{96,0},{97,1},{98,2},{99,3},{4,4},{5,5},{6,6},{7,7},{40,8},{41,9},... | collective-permute-start | bytes 393224 | tf_op jit(solution)/shard_map/ppermute | solution.py:172
  28.9 5.5 %collective-permute-start.1 = (f32[2048,128]{1,0:T(8,128)S(1)}, f32[2048,128]{1,0:T(8,128)S(1)}, u32[]{:S(2)}, u32[]{:S(2)}) collective-permute-start(f32[2048,128]{1,0:T(8,128)S(1)} %copy-done), channel_id=1, source_target_pairs={{0,1},{1,0},{2,3},{3,2},{4,5},{5,4},{6,7},{7,6},{8,9},{9,8},{10,11... | collective-permute-start | bytes 3145736 | tf_op jit(solution)/shard_map/ppermute | solution.py:179

commit v6 on v5

--- a/solution.py
+++ b/solution.py
@@ -39,7 +39,7 @@
 
 def rank(index):
     _, y, z, _ = place(index)
-    return z < Z_LO, (y - 4) % CHIPS_Y
+    return z < Z_LO, (y - 5) % CHIPS_Y
 
 
 TEAMS = [sorted(team, key=rank) for team in TEAMS.values()]

time: 51.6 us -> 51.3 us (level)
  blocking collectives: 35.4 us -> 34.8 us
where the time goes in v6:
time: 51.3 us; the launch traced here: 51 us
  blocking collectives  34.8 us (68%)
  starting transfers between devices  10.1 us (20%)
  Pallas kernels  5.01 us (10%)
  local copies, waits for them, and re-layouts  0.8 us (2%)
    all_to_all x1, blocking collectives, shards(): lax.all_to_all(copies, AXES, 0, 0, axis_index_groups=TEAMS)  21 us
    all_to_all x1, blocking collectives, shards(): parts = lax.all_to_all(part, AXES, 0, 0, axis_index_groups=TEAMS)  13.9 us
    pallas_call x6, Pallas kernels, call(): pl.pallas_call(kernel, out_shape=shapes, in_specs=[pl.BlockSpec(memory_sp...  5.01 us
    ppermute x1, starting transfers between devices, shards(): far = lax.ppermute(pts, AXES, FAR)  4.62 us
    ppermute x1, starting transfers between devices, shards(): other = lax.ppermute(slab_later, AXES, SWAP)  3.59 us
    ppermute x1, starting transfers between devices, shards(): near = lax.ppermute(pts, AXES, NEAR)  1.92 us
  transfers between devices with their start and end apart: 3, of which 1 were waited for; matrix products, arithmetic and copies ran while one was open for 0% of the time, Pallas kernels for 7%

profile of v6, /device:TPU:1, one launch (start us, length us, event | category | flops | bytes accessed | tf_op | source)
XLA Modules:
  0.0 51.0 jit_solution(12214015681629322941)
XLA Ops:
  0.0 0.0 copy-start
  0.0 0.8 %broadcast_in_dim.2 = f32[16,16,128]{2,1,0:T(8,128)S(1)} broadcast(f32[16,128]{1,0:T(8,128)} %param.2), dimensions={1,2} | broadcast | bytes 139264 | tf_op jit(solution)/shard_map/broadcast_in_dim | solution.py:169
  0.8 21.0 %all_to_all.10 = f32[16,16,128]{2,1,0:T(8,128)S(1)} all-to-all(f32[16,16,128]{2,1,0:T(8,128)S(1)} %broadcast_in_dim.2), channel_id=1, replica_groups={{278,282,286,258,262,266,270,274,20,24,28,0,4,8,12,16},{279,283,287,259..., dimensions={0} | all-to-all | bytes 262144 | tf_op jit(solution)/shard_map/all_to_all | solution.py:170
  21.8 4.6 %collective-permute-start.2 = (f32[256,128]{1,0:T(8,128)S(1)}, f32[256,128]{1,0:T(8,128)S(1)}, u32[]{:S(2)}, u32[]{:S(2)}) collective-permute-start(f32[256,128]{1,0:T(8,128)S(1)} %bitcast.1), channel_id=1, source_target_pairs={{192,0},{193,1},{194,2},{195,3},{164,4},{165,5},{166,6},{167,7},{1... | collective-permute-start | bytes 393224 | tf_op jit(solution)/shard_map/ppermute | solution.py:171
  26.4 1.9 %collective-permute-start = (f32[256,128]{1,0:T(8,128)S(1)}, f32[256,128]{1,0:T(8,128)S(1)}, u32[]{:S(2)}, u32[]{:S(2)}) collective-permute-start(f32[256,128]{1,0:T(8,128)S(1)} %bitcast.2), channel_id=1, source_target_pairs={{96,0},{97,1},{98,2},{99,3},{4,4},{5,5},{6,6},{7,7},{40,8},{41,9},... | collective-permute-start | bytes 393224 | tf_op jit(solution)/shard_map/ppermute | solution.py:172
  28.3 0.1 shard_map.28
  28.4 0.0 copy-done
  28.5 3.6 %collective-permute-start.1 = (f32[2048,128]{1,0:T(8,128)S(1)}, f32[2048,128]{1,0:T(8,128)S(1)}, u32[]{:S(2)}, u32[]{:S(2)}) collective-permute-start(f32[2048,128]{1,0:T(8,128)S(1)} %copy-done), channel_id=1, source_target_pairs={{0,1},{1,0},{2,3},{3,2},{4,5},{5,4},{6,7},{7,6},{8,9},{9,8},{10,11... | collective-permute-start | bytes 3145736 | tf_op jit(solution)/shard_map/ppermute | solution.py:179
  32.1 1.5 %shard_map.29 = (f32[256,128]{1,0:T(8,128)S(1)}, f32[256,128]{1,0:T(8,128)S(1)}) custom-call(bf16[256,256]{1,0:T(8,128)(2,1)S(1)} %get-tuple-element.18.left1_ref, bf16[256,256]{1,0:T(8,128)(2,1)S(1)} %get-tuple-element.19.left2_ref, f32[2048,128]{1,0:T(8,128)S(1)} %copy-done), custom_call_target="tpu_custom_call" | custom-call | flops 17179869184 | bytes 1024 | tf_op jit(solution)/shard_map/pallas_call | solution.py:155
  33.5 0.0 collective-permute-done.2.rows_ref
  33.6 0.6 %shard_map.30 = (f32[256,128]{1,0:T(8,128)S(1)}, f32[256,128]{1,0:T(8,128)S(1)}) custom-call(bf16[256,256]{1,0:T(8,128)(2,1)S(1)} %get-tuple-element.18.left1_ref, bf16[256,256]{1,0:T(8,128)(2,1)S(1)} %get-tuple-element.19.left2_ref, f32[256,128]{1,0:T(8,128)S(1)} %collective-permute-done.2.rows_ref), custom_call_target="tpu_custom_call" | custom-call | flops 2147483648 | bytes 1024 | tf_op jit(solution)/shard_map/pallas_call | solution.py:155
  34.2 0.2 collective-permute-done.1.rows_ref
  34.3 1.5 %shard_map.31 = (f32[256,128]{1,0:T(8,128)S(1)}, f32[256,128]{1,0:T(8,128)S(1)}) custom-call(bf16[256,256]{1,0:T(8,128)(2,1)S(1)} %get-tuple-element.18.left1_ref, bf16[256,256]{1,0:T(8,128)(2,1)S(1)} %get-tuple-element.19.left2_ref, f32[2048,128]{1,0:T(8,128)S(1)} %collective-permute-done.1.rows_ref), custom_call_target="tpu_custom_call" | custom-call | flops 2147483648 | bytes 1024 | tf_op jit(solution)/shard_map/pallas_call | solution.py:155
  35.8 0.0 collective-permute-done.rows_ref
  35.8 0.6 %shard_map.32 = f32[16,17,1,128]{3,2,1,0:T(1,128)S(1)} custom-call(f32[256,128]{1,0:T(8,128)S(1)} %bitcast.4, bf16[256,256]{1,0:T(8,128)(2,1)S(1)} %get-tuple-element.18.left1_ref, bf16[256,256]{1,0:T(8,128)(2,1)S(1)} %get-tuple-element.19.left2_ref, f32[256,128]{1,0:T(8,128)S(1)} %collective-permute-done.rows_ref, ...), custom_call_target="tpu_custom_call" | custom-call | flops 268435456 | bytes 1024 | tf_op jit(solution)/shard_map/pallas_call | solution.py:155
  36.5 13.9 %all_to_all.11.parts_ref = f32[16,17,1,128]{3,2,1,0:T(1,128)S(1)} all-to-all(f32[16,17,1,128]{3,2,1,0:T(1,128)S(1)} %shard_map.32), channel_id=1, replica_groups={{278,282,286,258,262,266,270,274,20,24,28,0,4,8,12,16},{279,283,287,259..., dimensions={0} | all-to-all | bytes 278528 | tf_op jit(solution)/shard_map/all_to_all | solution.py:188
  50.3 0.7 %shard_map.33 = f32[16,128]{1,0:T(8,128)} custom-call(f32[16,17,1,128]{3,2,1,0:T(1,128)S(1)} %all_to_all.11.parts_ref), custom_call_target="tpu_custom_call" | custom-call | flops 65536 | bytes 1024 | tf_op jit(solution)/shard_map/pallas_call | solution.py:155
Async XLA Ops:
  0.0 28.5 %copy-start = (f32[2048,128]{1,0:T(8,128)S(1)}, f32[2048,128]{1,0:T(8,128)}, u32[]{:S(2)}) copy-start(f32[2048,128]{1,0:T(8,128)} %rows_ref.1) | copy-start | bytes 3145732
  21.8 11.8 %collective-permute-start.2 = (f32[256,128]{1,0:T(8,128)S(1)}, f32[256,128]{1,0:T(8,128)S(1)}, u32[]{:S(2)}, u32[]{:S(2)}) collective-permute-start(f32[256,128]{1,0:T(8,128)S(1)} %bitcast.1), channel_id=1, source_target_pairs={{192,0},{193,1},{194,2},{195,3},{164,4},{165,5},{166,6},{167,7},{1... | collective-permute-start | bytes 393224 | tf_op jit(solution)/shard_map/ppermute | solution.py:171
  26.4 9.4 %collective-permute-start = (f32[256,128]{1,0:T(8,128)S(1)}, f32[256,128]{1,0:T(8,128)S(1)}, u32[]{:S(2)}, u32[]{:S(2)}) collective-permute-start(f32[256,128]{1,0:T(8,128)S(1)} %bitcast.2), channel_id=1, source_target_pairs={{96,0},{97,1},{98,2},{99,3},{4,4},{5,5},{6,6},{7,7},{40,8},{41,9},... | collective-permute-start | bytes 393224 | tf_op jit(solution)/shard_map/ppermute | solution.py:172
  28.5 5.9 %collective-permute-start.1 = (f32[2048,128]{1,0:T(8,128)S(1)}, f32[2048,128]{1,0:T(8,128)S(1)}, u32[]{:S(2)}, u32[]{:S(2)}) collective-permute-start(f32[2048,128]{1,0:T(8,128)S(1)} %copy-done), channel_id=1, source_target_pairs={{0,1},{1,0},{2,3},{3,2},{4,5},{5,4},{6,7},{7,6},{8,9},{9,8},{10,11... | collective-permute-start | bytes 3145736 | tf_op jit(solution)/shard_map/ppermute | solution.py:179

commit v7 on v6

--- a/solution.py
+++ b/solution.py
@@ -44,8 +44,8 @@
 
 TEAMS = [sorted(team, key=rank) for team in TEAMS.values()]
 
-X_FAR = ((2, 1, 0, 3), (1, 2, 3, 0), (0, 3, 2, 1), (3, 0, 1, 2))
-X_NEAR = ((3, 0, 1, 2), (0, 3, 2, 1), (1, 2, 3, 0), (2, 1, 0, 3))
+X_FAR = ((1, 2, 3, 0), (0, 3, 2, 1), (3, 0, 1, 2), (2, 1, 0, 3))
+X_NEAR = ((0, 3, 2, 1), (1, 2, 3, 0), (2, 1, 0, 3), (3, 0, 1, 2))
 Z_FAR, Z_NEAR = (1, 3, 0, 2, 5, 7, 4, 6), (0, 2, 1, 3, 4, 6, 5, 7)
 
 

time: 51.3 us -> 51.3 us (level)
  blocking collectives: 34.8 us -> 36.4 us
  starting transfers between devices: 10.1 us -> 8.62 us
    all_to_all x1, blocking collectives: 13.9 us -> 15.4 us  [shards(): parts = lax.all_to_all(part, AXES, 0, 0, axis_index_groups=TEAMS)]
    ppermute x1, starting transfers between devices: 1.92 us -> 0.67 us  [shards(): near = lax.ppermute(pts, AXES, NEAR)]
where the time goes in v7:
time: 51.3 us; the launch traced here: 51 us
  blocking collectives  36.4 us (71%)
  starting transfers between devices  8.62 us (17%)
  Pallas kernels  5.01 us (10%)
  local copies, waits for them, and re-layouts  0.8 us (2%)
    all_to_all x1, blocking collectives, shards(): lax.all_to_all(copies, AXES, 0, 0, axis_index_groups=TEAMS)  21 us
    all_to_all x1, blocking collectives, shards(): parts = lax.all_to_all(part, AXES, 0, 0, axis_index_groups=TEAMS)  15.4 us
    pallas_call x6, Pallas kernels, call(): pl.pallas_call(kernel, out_shape=shapes, in_specs=[pl.BlockSpec(memory_sp...  5.01 us
    ppermute x1, starting transfers between devices, shards(): far = lax.ppermute(pts, AXES, FAR)  4.35 us
    ppermute x1, starting transfers between devices, shards(): other = lax.ppermute(slab_later, AXES, SWAP)  3.59 us
  transfers between devices with their start and end apart: 3, of which 1 were waited for; matrix products, arithmetic and copies ran while one was open for 0% of the time, Pallas kernels for 7%

profile of v7, /device:TPU:1, one launch (start us, length us, event | category | flops | bytes accessed | tf_op | source)
XLA Modules:
  0.0 51.0 jit_solution(17352608521703201971)
XLA Ops:
  0.0 0.0 copy-start
  0.0 0.8 %broadcast_in_dim.2 = f32[16,16,128]{2,1,0:T(8,128)S(1)} broadcast(f32[16,128]{1,0:T(8,128)} %param.2), dimensions={1,2} | broadcast | bytes 139264 | tf_op jit(solution)/shard_map/broadcast_in_dim | solution.py:169
  0.8 21.0 %all_to_all.10 = f32[16,16,128]{2,1,0:T(8,128)S(1)} all-to-all(f32[16,16,128]{2,1,0:T(8,128)S(1)} %broadcast_in_dim.2), channel_id=1, replica_groups={{278,282,286,258,262,266,270,274,20,24,28,0,4,8,12,16},{279,283,287,259..., dimensions={0} | all-to-all | bytes 262144 | tf_op jit(solution)/shard_map/all_to_all | solution.py:170
  21.8 4.4 %collective-permute-start.2 = (f32[256,128]{1,0:T(8,128)S(1)}, f32[256,128]{1,0:T(8,128)S(1)}, u32[]{:S(2)}, u32[]{:S(2)}) collective-permute-start(f32[256,128]{1,0:T(8,128)S(1)} %bitcast.1), channel_id=1, source_target_pairs={{160,0},{161,1},{162,2},{163,3},{132,4},{133,5},{134,6},{135,7},{2... | collective-permute-start | bytes 393224 | tf_op jit(solution)/shard_map/ppermute | solution.py:171
  26.1 0.7 %collective-permute-start = (f32[256,128]{1,0:T(8,128)S(1)}, f32[256,128]{1,0:T(8,128)S(1)}, u32[]{:S(2)}, u32[]{:S(2)}) collective-permute-start(f32[256,128]{1,0:T(8,128)S(1)} %bitcast.2), channel_id=1, source_target_pairs={{0,0},{1,1},{2,2},{3,3},{36,4},{37,5},{38,6},{39,7},{72,8},{73,9},... | collective-permute-start | bytes 393224 | tf_op jit(solution)/shard_map/ppermute | solution.py:172
  26.8 0.1 shard_map.28
  26.9 0.0 copy-done
  26.9 3.6 %collective-permute-start.1 = (f32[2048,128]{1,0:T(8,128)S(1)}, f32[2048,128]{1,0:T(8,128)S(1)}, u32[]{:S(2)}, u32[]{:S(2)}) collective-permute-start(f32[2048,128]{1,0:T(8,128)S(1)} %copy-done), channel_id=1, source_target_pairs={{0,1},{1,0},{2,3},{3,2},{4,5},{5,4},{6,7},{7,6},{8,9},{9,8},{10,11... | collective-permute-start | bytes 3145736 | tf_op jit(solution)/shard_map/ppermute | solution.py:179
  30.5 1.5 %shard_map.29 = (f32[256,128]{1,0:T(8,128)S(1)}, f32[256,128]{1,0:T(8,128)S(1)}) custom-call(bf16[256,256]{1,0:T(8,128)(2,1)S(1)} %get-tuple-element.18.left1_ref, bf16[256,256]{1,0:T(8,128)(2,1)S(1)} %get-tuple-element.19.left2_ref, f32[2048,128]{1,0:T(8,128)S(1)} %copy-done), custom_call_target="tpu_custom_call" | custom-call | flops 17179869184 | bytes 1024 | tf_op jit(solution)/shard_map/pallas_call | solution.py:155
  32.0 0.0 collective-permute-done.2.rows_ref
  32.0 0.6 %shard_map.30 = (f32[256,128]{1,0:T(8,128)S(1)}, f32[256,128]{1,0:T(8,128)S(1)}) custom-call(bf16[256,256]{1,0:T(8,128)(2,1)S(1)} %get-tuple-element.18.left1_ref, bf16[256,256]{1,0:T(8,128)(2,1)S(1)} %get-tuple-element.19.left2_ref, f32[256,128]{1,0:T(8,128)S(1)} %collective-permute-done.2.rows_ref), custom_call_target="tpu_custom_call" | custom-call | flops 2147483648 | bytes 1024 | tf_op jit(solution)/shard_map/pallas_call | solution.py:155
  32.6 0.2 collective-permute-done.1.rows_ref
  32.8 1.5 %shard_map.31 = (f32[256,128]{1,0:T(8,128)S(1)}, f32[256,128]{1,0:T(8,128)S(1)}) custom-call(bf16[256,256]{1,0:T(8,128)(2,1)S(1)} %get-tuple-element.18.left1_ref, bf16[256,256]{1,0:T(8,128)(2,1)S(1)} %get-tuple-element.19.left2_ref, f32[2048,128]{1,0:T(8,128)S(1)} %collective-permute-done.1.rows_ref), custom_call_target="tpu_custom_call" | custom-call | flops 2147483648 | bytes 1024 | tf_op jit(solution)/shard_map/pallas_call | solution.py:155
  34.3 0.0 collective-permute-done.rows_ref
  34.3 0.6 %shard_map.32 = f32[16,17,1,128]{3,2,1,0:T(1,128)S(1)} custom-call(f32[256,128]{1,0:T(8,128)S(1)} %bitcast.4, bf16[256,256]{1,0:T(8,128)(2,1)S(1)} %get-tuple-element.18.left1_ref, bf16[256,256]{1,0:T(8,128)(2,1)S(1)} %get-tuple-element.19.left2_ref, f32[256,128]{1,0:T(8,128)S(1)} %collective-permute-done.rows_ref, ...), custom_call_target="tpu_custom_call" | custom-call | flops 268435456 | bytes 1024 | tf_op jit(solution)/shard_map/pallas_call | solution.py:155
  34.9 15.4 %all_to_all.11.parts_ref = f32[16,17,1,128]{3,2,1,0:T(1,128)S(1)} all-to-all(f32[16,17,1,128]{3,2,1,0:T(1,128)S(1)} %shard_map.32), channel_id=1, replica_groups={{278,282,286,258,262,266,270,274,20,24,28,0,4,8,12,16},{279,283,287,259..., dimensions={0} | all-to-all | bytes 278528 | tf_op jit(solution)/shard_map/all_to_all | solution.py:188
  50.3 0.7 %shard_map.33 = f32[16,128]{1,0:T(8,128)} custom-call(f32[16,17,1,128]{3,2,1,0:T(1,128)S(1)} %all_to_all.11.parts_ref), custom_call_target="tpu_custom_call" | custom-call | flops 65536 | bytes 1024 | tf_op jit(solution)/shard_map/pallas_call | solution.py:155
Async XLA Ops:
  0.0 26.9 %copy-start = (f32[2048,128]{1,0:T(8,128)S(1)}, f32[2048,128]{1,0:T(8,128)}, u32[]{:S(2)}) copy-start(f32[2048,128]{1,0:T(8,128)} %rows_ref.1) | copy-start | bytes 3145732
  21.8 10.3 %collective-permute-start.2 = (f32[256,128]{1,0:T(8,128)S(1)}, f32[256,128]{1,0:T(8,128)S(1)}, u32[]{:S(2)}, u32[]{:S(2)}) collective-permute-start(f32[256,128]{1,0:T(8,128)S(1)} %bitcast.1), channel_id=1, source_target_pairs={{160,0},{161,1},{162,2},{163,3},{132,4},{133,5},{134,6},{135,7},{2... | collective-permute-start | bytes 393224 | tf_op jit(solution)/shard_map/ppermute | solution.py:171
  26.1 8.2 %collective-permute-start = (f32[256,128]{1,0:T(8,128)S(1)}, f32[256,128]{1,0:T(8,128)S(1)}, u32[]{:S(2)}, u32[]{:S(2)}) collective-permute-start(f32[256,128]{1,0:T(8,128)S(1)} %bitcast.2), channel_id=1, source_target_pairs={{0,0},{1,1},{2,2},{3,3},{36,4},{37,5},{38,6},{39,7},{72,8},{73,9},... | collective-permute-start | bytes 393224 | tf_op jit(solution)/shard_map/ppermute | solution.py:172
  26.9 5.9 %collective-permute-start.1 = (f32[2048,128]{1,0:T(8,128)S(1)}, f32[2048,128]{1,0:T(8,128)S(1)}, u32[]{:S(2)}, u32[]{:S(2)}) collective-permute-start(f32[2048,128]{1,0:T(8,128)S(1)} %copy-done), channel_id=1, source_target_pairs={{0,1},{1,0},{2,3},{3,2},{4,5},{5,4},{6,7},{7,6},{8,9},{9,8},{10,11... | collective-permute-start | bytes 3145736 | tf_op jit(solution)/shard_map/ppermute | solution.py:179

commit v8 on v7

--- a/solution.py
+++ b/solution.py
@@ -46,7 +46,7 @@
 
 X_FAR = ((1, 2, 3, 0), (0, 3, 2, 1), (3, 0, 1, 2), (2, 1, 0, 3))
 X_NEAR = ((0, 3, 2, 1), (1, 2, 3, 0), (2, 1, 0, 3), (3, 0, 1, 2))
-Z_FAR, Z_NEAR = (1, 3, 0, 2, 5, 7, 4, 6), (0, 2, 1, 3, 4, 6, 5, 7)
+Z_FAR, Z_NEAR = (2, 0, 3, 1, 6, 4, 7, 5), (0, 2, 1, 3, 4, 6, 5, 7)
 
 
 def cross(x_orders, z_order):

time: 51.3 us -> 53.6 us (1.045)
  blocking collectives: 36.4 us -> 37.7 us
  starting transfers between devices: 8.62 us -> 9.55 us
    all_to_all x1, blocking collectives: 15.4 us -> 16.7 us  [shards(): parts = lax.all_to_all(part, AXES, 0, 0, axis_index_groups=TEAMS)]
    ppermute x1, starting transfers between devices: 4.35 us -> 5.28 us  [shards(): far = lax.ppermute(pts, AXES, FAR)]
where the time goes in v8:
time: 53.6 us; the launch traced here: 53.3 us
  blocking collectives  37.7 us (70%)
  starting transfers between devices  9.55 us (18%)
  Pallas kernels  5.01 us (9%)
  local copies, waits for them, and re-layouts  0.8 us (1%)
    all_to_all x1, blocking collectives, shards(): lax.all_to_all(copies, AXES, 0, 0, axis_index_groups=TEAMS)  21 us
    all_to_all x1, blocking collectives, shards(): parts = lax.all_to_all(part, AXES, 0, 0, axis_index_groups=TEAMS)  16.7 us
    ppermute x1, starting transfers between devices, shards(): far = lax.ppermute(pts, AXES, FAR)  5.28 us
    pallas_call x6, Pallas kernels, call(): pl.pallas_call(kernel, out_shape=shapes, in_specs=[pl.BlockSpec(memory_sp...  5.01 us
    ppermute x1, starting transfers between devices, shards(): other = lax.ppermute(slab_later, AXES, SWAP)  3.59 us
  transfers between devices with their start and end apart: 3, of which 1 were waited for; matrix products, arithmetic and copies ran while one was open for 0% of the time, Pallas kernels for 7%

profile of v8, /device:TPU:1, one launch (start us, length us, event | category | flops | bytes accessed | tf_op | source)
XLA Modules:
  0.0 53.3 jit_solution(8304446817404243575)
XLA Ops:
  0.0 0.0 copy-start
  0.0 0.8 %broadcast_in_dim.2 = f32[16,16,128]{2,1,0:T(8,128)S(1)} broadcast(f32[16,128]{1,0:T(8,128)} %param.2), dimensions={1,2} | broadcast | bytes 139264 | tf_op jit(solution)/shard_map/broadcast_in_dim | solution.py:169
  0.8 21.0 %all_to_all.10 = f32[16,16,128]{2,1,0:T(8,128)S(1)} all-to-all(f32[16,16,128]{2,1,0:T(8,128)S(1)} %broadcast_in_dim.2), channel_id=1, replica_groups={{278,282,286,258,262,266,270,274,20,24,28,0,4,8,12,16},{279,283,287,259..., dimensions={0} | all-to-all | bytes 262144 | tf_op jit(solution)/shard_map/all_to_all | solution.py:170
  21.8 5.3 %collective-permute-start.2 = (f32[256,128]{1,0:T(8,128)S(1)}, f32[256,128]{1,0:T(8,128)S(1)}, u32[]{:S(2)}, u32[]{:S(2)}) collective-permute-start(f32[256,128]{1,0:T(8,128)S(1)} %bitcast.1), channel_id=1, source_target_pairs={{288,0},{289,1},{290,2},{291,3},{260,4},{261,5},{262,6},{263,7},{3... | collective-permute-start | bytes 393224 | tf_op jit(solution)/shard_map/ppermute | solution.py:171
  27.1 0.7 %collective-permute-start = (f32[256,128]{1,0:T(8,128)S(1)}, f32[256,128]{1,0:T(8,128)S(1)}, u32[]{:S(2)}, u32[]{:S(2)}) collective-permute-start(f32[256,128]{1,0:T(8,128)S(1)} %bitcast.2), channel_id=1, source_target_pairs={{0,0},{1,1},{2,2},{3,3},{36,4},{37,5},{38,6},{39,7},{72,8},{73,9},... | collective-permute-start | bytes 393224 | tf_op jit(solution)/shard_map/ppermute | solution.py:172
  27.7 0.1 shard_map.28
  27.9 0.0 copy-done
  27.9 3.6 %collective-permute-start.1 = (f32[2048,128]{1,0:T(8,128)S(1)}, f32[2048,128]{1,0:T(8,128)S(1)}, u32[]{:S(2)}, u32[]{:S(2)}) collective-permute-start(f32[2048,128]{1,0:T(8,128)S(1)} %copy-done), channel_id=1, source_target_pairs={{0,1},{1,0},{2,3},{3,2},{4,5},{5,4},{6,7},{7,6},{8,9},{9,8},{10,11... | collective-permute-start | bytes 3145736 | tf_op jit(solution)/shard_map/ppermute | solution.py:179
  31.5 1.5 %shard_map.29 = (f32[256,128]{1,0:T(8,128)S(1)}, f32[256,128]{1,0:T(8,128)S(1)}) custom-call(bf16[256,256]{1,0:T(8,128)(2,1)S(1)} %get-tuple-element.18.left1_ref, bf16[256,256]{1,0:T(8,128)(2,1)S(1)} %get-tuple-element.19.left2_ref, f32[2048,128]{1,0:T(8,128)S(1)} %copy-done), custom_call_target="tpu_custom_call" | custom-call | flops 17179869184 | bytes 1024 | tf_op jit(solution)/shard_map/pallas_call | solution.py:155
  33.0 0.0 collective-permute-done.2.rows_ref
  33.0 0.6 %shard_map.30 = (f32[256,128]{1,0:T(8,128)S(1)}, f32[256,128]{1,0:T(8,128)S(1)}) custom-call(bf16[256,256]{1,0:T(8,128)(2,1)S(1)} %get-tuple-element.18.left1_ref, bf16[256,256]{1,0:T(8,128)(2,1)S(1)} %get-tuple-element.19.left2_ref, f32[256,128]{1,0:T(8,128)S(1)} %collective-permute-done.2.rows_ref), custom_call_target="tpu_custom_call" | custom-call | flops 2147483648 | bytes 1024 | tf_op jit(solution)/shard_map/pallas_call | solution.py:155
  33.6 0.2 collective-permute-done.1.rows_ref
  33.7 1.5 %shard_map.31 = (f32[256,128]{1,0:T(8,128)S(1)}, f32[256,128]{1,0:T(8,128)S(1)}) custom-call(bf16[256,256]{1,0:T(8,128)(2,1)S(1)} %get-tuple-element.18.left1_ref, bf16[256,256]{1,0:T(8,128)(2,1)S(1)} %get-tuple-element.19.left2_ref, f32[2048,128]{1,0:T(8,128)S(1)} %collective-permute-done.1.rows_ref), custom_call_target="tpu_custom_call" | custom-call | flops 2147483648 | bytes 1024 | tf_op jit(solution)/shard_map/pallas_call | solution.py:155
  35.2 0.0 collective-permute-done.rows_ref
  35.2 0.6 %shard_map.32 = f32[16,17,1,128]{3,2,1,0:T(1,128)S(1)} custom-call(f32[256,128]{1,0:T(8,128)S(1)} %bitcast.4, bf16[256,256]{1,0:T(8,128)(2,1)S(1)} %get-tuple-element.18.left1_ref, bf16[256,256]{1,0:T(8,128)(2,1)S(1)} %get-tuple-element.19.left2_ref, f32[256,128]{1,0:T(8,128)S(1)} %collective-permute-done.rows_ref, ...), custom_call_target="tpu_custom_call" | custom-call | flops 268435456 | bytes 1024 | tf_op jit(solution)/shard_map/pallas_call | solution.py:155
  35.9 16.7 %all_to_all.11.parts_ref = f32[16,17,1,128]{3,2,1,0:T(1,128)S(1)} all-to-all(f32[16,17,1,128]{3,2,1,0:T(1,128)S(1)} %shard_map.32), channel_id=1, replica_groups={{278,282,286,258,262,266,270,274,20,24,28,0,4,8,12,16},{279,283,287,259..., dimensions={0} | all-to-all | bytes 278528 | tf_op jit(solution)/shard_map/all_to_all | solution.py:188
  52.6 0.7 %shard_map.33 = f32[16,128]{1,0:T(8,128)} custom-call(f32[16,17,1,128]{3,2,1,0:T(1,128)S(1)} %all_to_all.11.parts_ref), custom_call_target="tpu_custom_call" | custom-call | flops 65536 | bytes 1024 | tf_op jit(solution)/shard_map/pallas_call | solution.py:155
Async XLA Ops:
  0.0 27.9 %copy-start = (f32[2048,128]{1,0:T(8,128)S(1)}, f32[2048,128]{1,0:T(8,128)}, u32[]{:S(2)}) copy-start(f32[2048,128]{1,0:T(8,128)} %rows_ref.1) | copy-start | bytes 3145732
  21.8 11.2 %collective-permute-start.2 = (f32[256,128]{1,0:T(8,128)S(1)}, f32[256,128]{1,0:T(8,128)S(1)}, u32[]{:S(2)}, u32[]{:S(2)}) collective-permute-start(f32[256,128]{1,0:T(8,128)S(1)} %bitcast.1), channel_id=1, source_target_pairs={{288,0},{289,1},{290,2},{291,3},{260,4},{261,5},{262,6},{263,7},{3... | collective-permute-start | bytes 393224 | tf_op jit(solution)/shard_map/ppermute | solution.py:171
  27.1 8.2 %collective-permute-start = (f32[256,128]{1,0:T(8,128)S(1)}, f32[256,128]{1,0:T(8,128)S(1)}, u32[]{:S(2)}, u32[]{:S(2)}) collective-permute-start(f32[256,128]{1,0:T(8,128)S(1)} %bitcast.2), channel_id=1, source_target_pairs={{0,0},{1,1},{2,2},{3,3},{36,4},{37,5},{38,6},{39,7},{72,8},{73,9},... | collective-permute-start | bytes 393224 | tf_op jit(solution)/shard_map/ppermute | solution.py:172
  27.9 5.9 %collective-permute-start.1 = (f32[2048,128]{1,0:T(8,128)S(1)}, f32[2048,128]{1,0:T(8,128)S(1)}, u32[]{:S(2)}, u32[]{:S(2)}) collective-permute-start(f32[2048,128]{1,0:T(8,128)S(1)} %copy-done), channel_id=1, source_target_pairs={{0,1},{1,0},{2,3},{3,2},{4,5},{5,4},{6,7},{7,6},{8,9},{9,8},{10,11... | collective-permute-start | bytes 3145736 | tf_op jit(solution)/shard_map/ppermute | solution.py:179

commit v9 on v8

--- a/solution.py
+++ b/solution.py
@@ -46,7 +46,7 @@
 
 X_FAR = ((1, 2, 3, 0), (0, 3, 2, 1), (3, 0, 1, 2), (2, 1, 0, 3))
 X_NEAR = ((0, 3, 2, 1), (1, 2, 3, 0), (2, 1, 0, 3), (3, 0, 1, 2))
-Z_FAR, Z_NEAR = (2, 0, 3, 1, 6, 4, 7, 5), (0, 2, 1, 3, 4, 6, 5, 7)
+Z_FAR, Z_NEAR = (1, 3, 0, 2, 5, 6, 4, 7), (0, 2, 1, 3, 4, 7, 5, 6)
 
 
 def cross(x_orders, z_order):

time: 53.6 us -> 52.7 us (0.983)
  starting transfers between devices: 9.55 us -> 8.62 us
    ppermute x1, starting transfers between devices: 5.28 us -> 4.35 us  [shards(): far = lax.ppermute(pts, AXES, FAR)]
where the time goes in v9:
time: 52.7 us; the launch traced here: 52.4 us
  blocking collectives  37.7 us (72%)
  starting transfers between devices  8.62 us (16%)
  Pallas kernels  5.01 us (10%)
  local copies, waits for them, and re-layouts  0.8 us (2%)
    all_to_all x1, blocking collectives, shards(): lax.all_to_all(copies, AXES, 0, 0, axis_index_groups=TEAMS)  21 us
    all_to_all x1, blocking collectives, shards(): parts = lax.all_to_all(part, AXES, 0, 0, axis_index_groups=TEAMS)  16.7 us
    pallas_call x6, Pallas kernels, call(): pl.pallas_call(kernel, out_shape=shapes, in_specs=[pl.BlockSpec(memory_sp...  5.01 us
    ppermute x1, starting transfers between devices, shards(): far = lax.ppermute(pts, AXES, FAR)  4.35 us
    ppermute x1, starting transfers between devices, shards(): other = lax.ppermute(slab_later, AXES, SWAP)  3.59 us
  transfers between devices with their start and end apart: 3, of which 1 were waited for; matrix products, arithmetic and copies ran while one was open for 0% of the time, Pallas kernels for 7%

profile of v9, /device:TPU:1, one launch (start us, length us, event | category | flops | bytes accessed | tf_op | source)
XLA Modules:
  0.0 52.4 jit_solution(4669050497656434301)
XLA Ops:
  0.0 0.0 copy-start
  0.0 0.8 %broadcast_in_dim.2 = f32[16,16,128]{2,1,0:T(8,128)S(1)} broadcast(f32[16,128]{1,0:T(8,128)} %param.2), dimensions={1,2} | broadcast | bytes 139264 | tf_op jit(solution)/shard_map/broadcast_in_dim | solution.py:169
  0.8 21.0 %all_to_all.10 = f32[16,16,128]{2,1,0:T(8,128)S(1)} all-to-all(f32[16,16,128]{2,1,0:T(8,128)S(1)} %broadcast_in_dim.2), channel_id=1, replica_groups={{278,282,286,258,262,266,270,274,20,24,28,0,4,8,12,16},{279,283,287,259..., dimensions={0} | all-to-all | bytes 262144 | tf_op jit(solution)/shard_map/all_to_all | solution.py:170
  21.8 4.4 %collective-permute-start.2 = (f32[256,128]{1,0:T(8,128)S(1)}, f32[256,128]{1,0:T(8,128)S(1)}, u32[]{:S(2)}, u32[]{:S(2)}) collective-permute-start(f32[256,128]{1,0:T(8,128)S(1)} %bitcast.1), channel_id=1, source_target_pairs={{160,0},{161,1},{162,2},{163,3},{132,4},{133,5},{134,6},{135,7},{2... | collective-permute-start | bytes 393224 | tf_op jit(solution)/shard_map/ppermute | solution.py:171
  26.1 0.7 %collective-permute-start = (f32[256,128]{1,0:T(8,128)S(1)}, f32[256,128]{1,0:T(8,128)S(1)}, u32[]{:S(2)}, u32[]{:S(2)}) collective-permute-start(f32[256,128]{1,0:T(8,128)S(1)} %bitcast.2), channel_id=1, source_target_pairs={{0,0},{1,1},{2,2},{3,3},{36,4},{37,5},{38,6},{39,7},{72,8},{73,9},... | collective-permute-start | bytes 393224 | tf_op jit(solution)/shard_map/ppermute | solution.py:172
  26.8 0.1 shard_map.28
  26.9 0.0 copy-done
  26.9 3.6 %collective-permute-start.1 = (f32[2048,128]{1,0:T(8,128)S(1)}, f32[2048,128]{1,0:T(8,128)S(1)}, u32[]{:S(2)}, u32[]{:S(2)}) collective-permute-start(f32[2048,128]{1,0:T(8,128)S(1)} %copy-done), channel_id=1, source_target_pairs={{0,1},{1,0},{2,3},{3,2},{4,5},{5,4},{6,7},{7,6},{8,9},{9,8},{10,11... | collective-permute-start | bytes 3145736 | tf_op jit(solution)/shard_map/ppermute | solution.py:179
  30.5 1.5 %shard_map.29 = (f32[256,128]{1,0:T(8,128)S(1)}, f32[256,128]{1,0:T(8,128)S(1)}) custom-call(bf16[256,256]{1,0:T(8,128)(2,1)S(1)} %get-tuple-element.18.left1_ref, bf16[256,256]{1,0:T(8,128)(2,1)S(1)} %get-tuple-element.19.left2_ref, f32[2048,128]{1,0:T(8,128)S(1)} %copy-done), custom_call_target="tpu_custom_call" | custom-call | flops 17179869184 | bytes 1024 | tf_op jit(solution)/shard_map/pallas_call | solution.py:155
  32.0 0.0 collective-permute-done.2.rows_ref
  32.0 0.6 %shard_map.30 = (f32[256,128]{1,0:T(8,128)S(1)}, f32[256,128]{1,0:T(8,128)S(1)}) custom-call(bf16[256,256]{1,0:T(8,128)(2,1)S(1)} %get-tuple-element.18.left1_ref, bf16[256,256]{1,0:T(8,128)(2,1)S(1)} %get-tuple-element.19.left2_ref, f32[256,128]{1,0:T(8,128)S(1)} %collective-permute-done.2.rows_ref), custom_call_target="tpu_custom_call" | custom-call | flops 2147483648 | bytes 1024 | tf_op jit(solution)/shard_map/pallas_call | solution.py:155
  32.6 0.2 collective-permute-done.1.rows_ref
  32.8 1.5 %shard_map.31 = (f32[256,128]{1,0:T(8,128)S(1)}, f32[256,128]{1,0:T(8,128)S(1)}) custom-call(bf16[256,256]{1,0:T(8,128)(2,1)S(1)} %get-tuple-element.18.left1_ref, bf16[256,256]{1,0:T(8,128)(2,1)S(1)} %get-tuple-element.19.left2_ref, f32[2048,128]{1,0:T(8,128)S(1)} %collective-permute-done.1.rows_ref), custom_call_target="tpu_custom_call" | custom-call | flops 2147483648 | bytes 1024 | tf_op jit(solution)/shard_map/pallas_call | solution.py:155
  34.3 0.0 collective-permute-done.rows_ref
  34.3 0.6 %shard_map.32 = f32[16,17,1,128]{3,2,1,0:T(1,128)S(1)} custom-call(f32[256,128]{1,0:T(8,128)S(1)} %bitcast.4, bf16[256,256]{1,0:T(8,128)(2,1)S(1)} %get-tuple-element.18.left1_ref, bf16[256,256]{1,0:T(8,128)(2,1)S(1)} %get-tuple-element.19.left2_ref, f32[256,128]{1,0:T(8,128)S(1)} %collective-permute-done.rows_ref, ...), custom_call_target="tpu_custom_call" | custom-call | flops 268435456 | bytes 1024 | tf_op jit(solution)/shard_map/pallas_call | solution.py:155
  34.9 16.7 %all_to_all.11.parts_ref = f32[16,17,1,128]{3,2,1,0:T(1,128)S(1)} all-to-all(f32[16,17,1,128]{3,2,1,0:T(1,128)S(1)} %shard_map.32), channel_id=1, replica_groups={{278,282,286,258,262,266,270,274,20,24,28,0,4,8,12,16},{279,283,287,259..., dimensions={0} | all-to-all | bytes 278528 | tf_op jit(solution)/shard_map/all_to_all | solution.py:188
  51.7 0.7 %shard_map.33 = f32[16,128]{1,0:T(8,128)} custom-call(f32[16,17,1,128]{3,2,1,0:T(1,128)S(1)} %all_to_all.11.parts_ref), custom_call_target="tpu_custom_call" | custom-call | flops 65536 | bytes 1024 | tf_op jit(solution)/shard_map/pallas_call | solution.py:155
Async XLA Ops:
  0.0 26.9 %copy-start = (f32[2048,128]{1,0:T(8,128)S(1)}, f32[2048,128]{1,0:T(8,128)}, u32[]{:S(2)}) copy-start(f32[2048,128]{1,0:T(8,128)} %rows_ref.1) | copy-start | bytes 3145732
  21.8 10.3 %collective-permute-start.2 = (f32[256,128]{1,0:T(8,128)S(1)}, f32[256,128]{1,0:T(8,128)S(1)}, u32[]{:S(2)}, u32[]{:S(2)}) collective-permute-start(f32[256,128]{1,0:T(8,128)S(1)} %bitcast.1), channel_id=1, source_target_pairs={{160,0},{161,1},{162,2},{163,3},{132,4},{133,5},{134,6},{135,7},{2... | collective-permute-start | bytes 393224 | tf_op jit(solution)/shard_map/ppermute | solution.py:171
  26.1 8.2 %collective-permute-start = (f32[256,128]{1,0:T(8,128)S(1)}, f32[256,128]{1,0:T(8,128)S(1)}, u32[]{:S(2)}, u32[]{:S(2)}) collective-permute-start(f32[256,128]{1,0:T(8,128)S(1)} %bitcast.2), channel_id=1, source_target_pairs={{0,0},{1,1},{2,2},{3,3},{36,4},{37,5},{38,6},{39,7},{72,8},{73,9},... | collective-permute-start | bytes 393224 | tf_op jit(solution)/shard_map/ppermute | solution.py:172
  26.9 5.9 %collective-permute-start.1 = (f32[2048,128]{1,0:T(8,128)S(1)}, f32[2048,128]{1,0:T(8,128)S(1)}, u32[]{:S(2)}, u32[]{:S(2)}) collective-permute-start(f32[2048,128]{1,0:T(8,128)S(1)} %copy-done), channel_id=1, source_target_pairs={{0,1},{1,0},{2,3},{3,2},{4,5},{5,4},{6,7},{7,6},{8,9},{9,8},{10,11... | collective-permute-start | bytes 3145736 | tf_op jit(solution)/shard_map/ppermute | solution.py:179

commit v10 on v7

--- a/solution.py
+++ b/solution.py
@@ -44,8 +44,8 @@
 
 TEAMS = [sorted(team, key=rank) for team in TEAMS.values()]
 
-X_FAR = ((1, 2, 3, 0), (0, 3, 2, 1), (3, 0, 1, 2), (2, 1, 0, 3))
-X_NEAR = ((0, 3, 2, 1), (1, 2, 3, 0), (2, 1, 0, 3), (3, 0, 1, 2))
+X_FAR = ((0, 3, 2, 1), (3, 0, 1, 2), (2, 1, 0, 3), (1, 2, 3, 0))
+X_NEAR = ((1, 2, 3, 0), (2, 1, 0, 3), (3, 0, 1, 2), (0, 3, 2, 1))
 Z_FAR, Z_NEAR = (1, 3, 0, 2, 5, 7, 4, 6), (0, 2, 1, 3, 4, 6, 5, 7)
 
 

time: 51.3 us -> 51.3 us (level)
  blocking collectives: 36.4 us -> 33.7 us
  starting transfers between devices: 8.62 us -> 11.3 us
    ppermute x1, starting transfers between devices: 0.67 us -> 5.23 us  [shards(): near = lax.ppermute(pts, AXES, NEAR)]
    all_to_all x1, blocking collectives: 15.4 us -> 12.7 us  [shards(): parts = lax.all_to_all(part, AXES, 0, 0, axis_index_groups=TEAMS)]
    ppermute x1, starting transfers between devices: 4.35 us -> 2.16 us  [shards(): far = lax.ppermute(pts, AXES, FAR)]
where the time goes in v10:
time: 51.3 us; the launch traced here: 51 us
  blocking collectives  33.7 us (66%)
  starting transfers between devices  11.3 us (22%)
  Pallas kernels  5.01 us (10%)
  local copies, waits for them, and re-layouts  0.8 us (2%)
    all_to_all x1, blocking collectives, shards(): lax.all_to_all(copies, AXES, 0, 0, axis_index_groups=TEAMS)  21 us
    all_to_all x1, blocking collectives, shards(): parts = lax.all_to_all(part, AXES, 0, 0, axis_index_groups=TEAMS)  12.7 us
    ppermute x1, starting transfers between devices, shards(): near = lax.ppermute(pts, AXES, NEAR)  5.23 us
    pallas_call x6, Pallas kernels, call(): pl.pallas_call(kernel, out_shape=shapes, in_specs=[pl.BlockSpec(memory_sp...  5.01 us
    ppermute x1, starting transfers between devices, shards(): other = lax.ppermute(slab_later, AXES, SWAP)  3.87 us
    ppermute x1, starting transfers between devices, shards(): far = lax.ppermute(pts, AXES, FAR)  2.16 us
  transfers between devices with their start and end apart: 3, of which 1 were waited for; matrix products, arithmetic and copies ran while one was open for 0% of the time, Pallas kernels for 7%

profile of v10, /device:TPU:1, one launch (start us, length us, event | category | flops | bytes accessed | tf_op | source)
XLA Modules:
  0.0 51.0 jit_solution(11273565992726514833)
XLA Ops:
  0.0 0.0 copy-start
  0.0 0.8 %broadcast_in_dim.2 = f32[16,16,128]{2,1,0:T(8,128)S(1)} broadcast(f32[16,128]{1,0:T(8,128)} %param.2), dimensions={1,2} | broadcast | bytes 139264 | tf_op jit(solution)/shard_map/broadcast_in_dim | solution.py:169
  0.8 21.0 %all_to_all.10 = f32[16,16,128]{2,1,0:T(8,128)S(1)} all-to-all(f32[16,16,128]{2,1,0:T(8,128)S(1)} %broadcast_in_dim.2), channel_id=1, replica_groups={{278,282,286,258,262,266,270,274,20,24,28,0,4,8,12,16},{279,283,287,259..., dimensions={0} | all-to-all | bytes 262144 | tf_op jit(solution)/shard_map/all_to_all | solution.py:170
  21.8 2.2 %collective-permute-start.2 = (f32[256,128]{1,0:T(8,128)S(1)}, f32[256,128]{1,0:T(8,128)S(1)}, u32[]{:S(2)}, u32[]{:S(2)}) collective-permute-start(f32[256,128]{1,0:T(8,128)S(1)} %bitcast.1), channel_id=1, source_target_pairs={{128,0},{129,1},{130,2},{131,3},{228,4},{229,5},{230,6},{231,7},{2... | collective-permute-start | bytes 393224 | tf_op jit(solution)/shard_map/ppermute | solution.py:171
  23.9 5.2 %collective-permute-start = (f32[256,128]{1,0:T(8,128)S(1)}, f32[256,128]{1,0:T(8,128)S(1)}, u32[]{:S(2)}, u32[]{:S(2)}) collective-permute-start(f32[256,128]{1,0:T(8,128)S(1)} %bitcast.2), channel_id=1, source_target_pairs={{32,0},{33,1},{34,2},{35,3},{68,4},{69,5},{70,6},{71,7},{104,8},{1... | collective-permute-start | bytes 393224 | tf_op jit(solution)/shard_map/ppermute | solution.py:172
  29.2 0.1 shard_map.28
  29.3 0.0 copy-done
  29.3 3.9 %collective-permute-start.1 = (f32[2048,128]{1,0:T(8,128)S(1)}, f32[2048,128]{1,0:T(8,128)S(1)}, u32[]{:S(2)}, u32[]{:S(2)}) collective-permute-start(f32[2048,128]{1,0:T(8,128)S(1)} %copy-done), channel_id=1, source_target_pairs={{0,1},{1,0},{2,3},{3,2},{4,5},{5,4},{6,7},{7,6},{8,9},{9,8},{10,11... | collective-permute-start | bytes 3145736 | tf_op jit(solution)/shard_map/ppermute | solution.py:179
  33.2 1.5 %shard_map.29 = (f32[256,128]{1,0:T(8,128)S(1)}, f32[256,128]{1,0:T(8,128)S(1)}) custom-call(bf16[256,256]{1,0:T(8,128)(2,1)S(1)} %get-tuple-element.18.left1_ref, bf16[256,256]{1,0:T(8,128)(2,1)S(1)} %get-tuple-element.19.left2_ref, f32[2048,128]{1,0:T(8,128)S(1)} %copy-done), custom_call_target="tpu_custom_call" | custom-call | flops 17179869184 | bytes 1024 | tf_op jit(solution)/shard_map/pallas_call | solution.py:155
  34.7 0.0 collective-permute-done.2.rows_ref
  34.7 0.6 %shard_map.30 = (f32[256,128]{1,0:T(8,128)S(1)}, f32[256,128]{1,0:T(8,128)S(1)}) custom-call(bf16[256,256]{1,0:T(8,128)(2,1)S(1)} %get-tuple-element.18.left1_ref, bf16[256,256]{1,0:T(8,128)(2,1)S(1)} %get-tuple-element.19.left2_ref, f32[256,128]{1,0:T(8,128)S(1)} %collective-permute-done.2.rows_ref), custom_call_target="tpu_custom_call" | custom-call | flops 2147483648 | bytes 1024 | tf_op jit(solution)/shard_map/pallas_call | solution.py:155
  35.3 0.2 collective-permute-done.1.rows_ref
  35.5 1.5 %shard_map.31 = (f32[256,128]{1,0:T(8,128)S(1)}, f32[256,128]{1,0:T(8,128)S(1)}) custom-call(bf16[256,256]{1,0:T(8,128)(2,1)S(1)} %get-tuple-element.18.left1_ref, bf16[256,256]{1,0:T(8,128)(2,1)S(1)} %get-tuple-element.19.left2_ref, f32[2048,128]{1,0:T(8,128)S(1)} %collective-permute-done.1.rows_ref), custom_call_target="tpu_custom_call" | custom-call | flops 2147483648 | bytes 1024 | tf_op jit(solution)/shard_map/pallas_call | solution.py:155
  36.9 0.0 collective-permute-done.rows_ref
  37.0 0.6 %shard_map.32 = f32[16,17,1,128]{3,2,1,0:T(1,128)S(1)} custom-call(f32[256,128]{1,0:T(8,128)S(1)} %bitcast.4, bf16[256,256]{1,0:T(8,128)(2,1)S(1)} %get-tuple-element.18.left1_ref, bf16[256,256]{1,0:T(8,128)(2,1)S(1)} %get-tuple-element.19.left2_ref, f32[256,128]{1,0:T(8,128)S(1)} %collective-permute-done.rows_ref, ...), custom_call_target="tpu_custom_call" | custom-call | flops 268435456 | bytes 1024 | tf_op jit(solution)/shard_map/pallas_call | solution.py:155
  37.6 12.7 %all_to_all.11.parts_ref = f32[16,17,1,128]{3,2,1,0:T(1,128)S(1)} all-to-all(f32[16,17,1,128]{3,2,1,0:T(1,128)S(1)} %shard_map.32), channel_id=1, replica_groups={{278,282,286,258,262,266,270,274,20,24,28,0,4,8,12,16},{279,283,287,259..., dimensions={0} | all-to-all | bytes 278528 | tf_op jit(solution)/shard_map/all_to_all | solution.py:188
  50.3 0.7 %shard_map.33 = f32[16,128]{1,0:T(8,128)} custom-call(f32[16,17,1,128]{3,2,1,0:T(1,128)S(1)} %all_to_all.11.parts_ref), custom_call_target="tpu_custom_call" | custom-call | flops 65536 | bytes 1024 | tf_op jit(solution)/shard_map/pallas_call | solution.py:155
Async XLA Ops:
  0.0 29.3 %copy-start = (f32[2048,128]{1,0:T(8,128)S(1)}, f32[2048,128]{1,0:T(8,128)}, u32[]{:S(2)}) copy-start(f32[2048,128]{1,0:T(8,128)} %rows_ref.1) | copy-start | bytes 3145732
  21.8 12.9 %collective-permute-start.2 = (f32[256,128]{1,0:T(8,128)S(1)}, f32[256,128]{1,0:T(8,128)S(1)}, u32[]{:S(2)}, u32[]{:S(2)}) collective-permute-start(f32[256,128]{1,0:T(8,128)S(1)} %bitcast.1), channel_id=1, source_target_pairs={{128,0},{129,1},{130,2},{131,3},{228,4},{229,5},{230,6},{231,7},{2... | collective-permute-start | bytes 393224 | tf_op jit(solution)/shard_map/ppermute | solution.py:171
  23.9 13.0 %collective-permute-start = (f32[256,128]{1,0:T(8,128)S(1)}, f32[256,128]{1,0:T(8,128)S(1)}, u32[]{:S(2)}, u32[]{:S(2)}) collective-permute-start(f32[256,128]{1,0:T(8,128)S(1)} %bitcast.2), channel_id=1, source_target_pairs={{32,0},{33,1},{34,2},{35,3},{68,4},{69,5},{70,6},{71,7},{104,8},{1... | collective-permute-start | bytes 393224 | tf_op jit(solution)/shard_map/ppermute | solution.py:172
  29.3 6.1 %collective-permute-start.1 = (f32[2048,128]{1,0:T(8,128)S(1)}, f32[2048,128]{1,0:T(8,128)S(1)}, u32[]{:S(2)}, u32[]{:S(2)}) collective-permute-start(f32[2048,128]{1,0:T(8,128)S(1)} %copy-done), channel_id=1, source_target_pairs={{0,1},{1,0},{2,3},{3,2},{4,5},{5,4},{6,7},{7,6},{8,9},{9,8},{10,11... | collective-permute-start | bytes 3145736 | tf_op jit(solution)/shard_map/ppermute | solution.py:179
